TPU v7x, 128 devices: a whole 4x4x4 slice. The times are simulated.
128 devices in a mesh: tile: 8 (over x, core), mode: 16 (over z, y).
Axes of the slice: x: 4, y: 4, z: 4, core: 2. Of those that a mesh axis runs over, the one named last changes fastest.
Arguments:
- object_field: float32 [2, 2048, 512], P(None, 'tile'), may hold values from -3 to 3
- probe_modes: float32 [16, 2, 256, 256], P('mode'), may hold values from -3 to 3
- patterns: bfloat16 [64, 256, 256], P('tile'), may hold values from 0 to 16
- offsets: int32 [64, 2], P('tile'), may hold values from 0 to 256, as said below
- counts: int32 [8], P('tile'), may hold values from 1 to 8, as said below
Outputs:
- updated_object: float32 [2, 2048, 512], P(None, 'tile')
Inputs may be any that keep to these rules, and one draw needn't show every extreme that they name: `offsets`: column 0 is the patch's first row within its strip of 256 rows, column 1 its first column; a patch may reach into the next strip. Some slot starts at row 255 and column 256, some at row 0 and column 0. A strip's live slots are its first counts[t] slots; the other slots hold offsets and patterns that are not used. Some strip has 8 live slots.
All inputs are finite; a program needn't handle non-finite values.
Results may differ from a plain program's by a relative error of at most 0.003.
Values may be sent and summed in bfloat16 or wider, within the bound.
A program may use at most 128 MiB of HBM per device.

v0:
```python
import math

import jax
import jax.numpy as jnp
from jax import lax
from jax.sharding import PartitionSpec as P

PATCH = 256
PASSES = 2


STEP_SIZE = 0.9


def from_behind(x, axis, by):
    count = lax.axis_size(axis)
    pairs = [(i, i + by) for i in range(count) if 0 <= i + by < count]
    return lax.ppermute(x, axis, pairs)


def make_tables():
    indices = jnp.arange(PATCH, dtype=jnp.int32)
    product = indices[:, None] * indices[None, :] % PATCH
    angles = product.astype(jnp.float32) * (2.0 * math.pi / PATCH)
    factor = 1.0 / math.sqrt(PATCH)
    cosine = (jnp.cos(angles) * factor).astype(jnp.bfloat16)
    minus_sine = (-jnp.sin(angles) * factor).astype(jnp.bfloat16)
    first_table = jnp.stack([jnp.stack([cosine, -minus_sine]), jnp.stack([minus_sine, cosine])])
    second_table = jnp.stack([jnp.stack([cosine, minus_sine]), jnp.stack([-minus_sine, cosine])])
    return (first_table, second_table)


def transform(values, first_table, second_table):
    halfway = jnp.einsum(
        "cdux,...dxy->...cuy", first_table, values, preferred_element_type=jnp.float32
    )
    halfway = halfway.astype(jnp.bfloat16)
    return jnp.einsum(
        "...dux,dcxy->...cuy", halfway, second_table, preferred_element_type=jnp.float32
    )


def apply_probe(probes, field):
    real_part = (
        probes[..., 0, :, :] * field[..., 0, :, :] - probes[..., 1, :, :] * field[..., 1, :, :]
    )
    imag_part = (
        probes[..., 0, :, :] * field[..., 1, :, :] + probes[..., 1, :, :] * field[..., 0, :, :]
    )
    return jnp.stack([real_part, imag_part], axis=-3)


def conj_probe(probes, field):
    real_part = (
        probes[..., 0, :, :] * field[..., 0, :, :] + probes[..., 1, :, :] * field[..., 1, :, :]
    )
    imag_part = (
        probes[..., 0, :, :] * field[..., 1, :, :] - probes[..., 1, :, :] * field[..., 0, :, :]
    )
    return jnp.stack([real_part, imag_part], axis=-3)


def coverage(offsets, counts, height, width):
    slot_count = offsets.shape[0]
    live_mask = (jnp.arange(slot_count, dtype=jnp.int32) < counts[0]).astype(jnp.float32)
    row_grid = jnp.arange(height, dtype=jnp.int32)[None, :, None]
    col_grid = jnp.arange(width, dtype=jnp.int32)[None, None, :]
    first_row = offsets[:, 0][:, None, None]
    first_col = offsets[:, 1][:, None, None]
    inside = (row_grid >= first_row) & (row_grid < first_row + PATCH)
    inside = inside & (col_grid >= first_col) & (col_grid < first_col + PATCH)
    return jnp.sum(inside.astype(jnp.float32) * live_mask[:, None, None], axis=0)


def shards(object_field, probe_modes, patterns, offsets, counts):
    first_table, second_table = make_tables()
    strip_rows = object_field.shape[1]
    width = object_field.shape[2]
    slot_count = offsets.shape[0]
    next_strip = from_behind(object_field.astype(jnp.bfloat16), "tile", -1).astype(
        object_field.dtype
    )
    extended = jnp.concatenate([object_field, next_strip], axis=1)
    probe_power = lax.psum(
        jnp.sum(probe_modes[:, 0] ** 2 + probe_modes[:, 1] ** 2, axis=0).astype(jnp.bfloat16),
        "mode",
    ).astype(jnp.float32)
    highest = jnp.max(probe_power)
    live_mask = (jnp.arange(slot_count, dtype=jnp.int32) < counts[0]).astype(jnp.float32)

    def cut_patch(row_start, col_start):
        return lax.dynamic_slice(extended, (jnp.int32(0), row_start, col_start), (2, PATCH, PATCH))

    initial = jax.vmap(cut_patch)(offsets[:, 0], offsets[:, 1])
    current = initial
    for repeat in range(PASSES):
        exit_wave = apply_probe(probe_modes, current).astype(jnp.bfloat16)
        far_field = transform(exit_wave, first_table, second_table)
        own_intensity = far_field[:, 0] ** 2 + far_field[:, 1] ** 2
        intensity = lax.psum(own_intensity.astype(jnp.bfloat16), "mode").astype(jnp.float32)
        amp_ratio = jnp.sqrt(patterns.astype(jnp.float32) / jnp.maximum(intensity, 1.0))
        far_change = ((amp_ratio[:, None] - 1.0) * far_field).astype(jnp.bfloat16)
        near_change = transform(far_change, second_table, first_table)
        mode_term = conj_probe(probe_modes, near_change)
        update = lax.psum(mode_term.astype(jnp.bfloat16), "mode").astype(jnp.float32)
        current = current + STEP_SIZE / highest * update
    moved = (current - initial) * live_mask[:, None, None, None]
    summed = jnp.zeros((2, strip_rows + PATCH, width), jnp.float32)
    for member in range(slot_count):
        row_start = offsets[member, 0]
        col_start = offsets[member, 1]
        piece = (
            lax.dynamic_slice(summed, (jnp.int32(0), row_start, col_start), (2, PATCH, PATCH))
            + moved[member]
        )
        summed = lax.dynamic_update_slice(summed, piece, (jnp.int32(0), row_start, col_start))
    covered = coverage(offsets, counts, strip_rows + PATCH, width)
    spilled, spilled_cover = (
        from_behind(summed[:, strip_rows:].astype(jnp.bfloat16), "tile", 1).astype(jnp.float32),
        from_behind(covered[strip_rows:].astype(jnp.bfloat16), "tile", 1).astype(jnp.float32),
    )
    spill_change = jnp.concatenate(
        [spilled, jnp.zeros((2, strip_rows - PATCH, width), jnp.float32)], axis=1
    )
    spill_count = jnp.concatenate(
        [spilled_cover, jnp.zeros((strip_rows - PATCH, width), jnp.float32)], axis=0
    )
    total_change = summed[:, :strip_rows] + spill_change
    total_cover = covered[:strip_rows] + spill_count
    return object_field + total_change / jnp.maximum(total_cover, 1.0)


def solution(mesh):
    return jax.shard_map(
        shards,
        mesh=mesh,
        in_specs=(
            P(None, "tile", None),
            P("mode", None, None, None),
            P("tile", None, None),
            P("tile", None),
            P("tile"),
        ),
        out_specs=P(None, "tile", None),
        check_vma=False,
    )
```

profile of v0, /device:TPU:6, one launch (start us, length us, event | category | flops | bytes accessed | tf_op | source)
XLA Modules:
  0.0 572.5 jit_solution(8942213237280289094)
XLA Ops:
  7.8 2.2 collective-permute-start
  17.0 24.9 %while.1 = (s32[]{:T(128)}, f32[2,512,512]{2,1,0:T(8,128)S(1)}, s32[8,3]{0,1:T(4,128)S(1)}, f32[8,2,256,256]{2,3,0,1:T(8,128)}, s32[]{:T(128)}) while((s32[]{:T(128)}, f32[2,512,512]{2,1,0:T(8,128)S(1)}, s32[8,3]{0,1:T(4,128)S(1)}, f32[8,2,256,256]{2,3,0,1:T(8,128)}, s32[]{:T(128)}) %tuple.49), condition=%wide.while_cond, body=%wide.while_body.sunk | while | flops 2 | bytes 3146353 | solution.py:92
  17.6 1.5 dynamic-slice_bitcast_fusion.2
  20.7 1.5 dynamic-slice_bitcast_fusion.2
  23.8 1.5 dynamic-slice_bitcast_fusion.2
  27.0 1.5 dynamic-slice_bitcast_fusion.2
  30.1 1.5 dynamic-slice_bitcast_fusion.2
  33.2 1.5 dynamic-slice_bitcast_fusion.2
  36.3 1.5 dynamic-slice_bitcast_fusion.2
  41.9 2.9 subtract_convert_fusion.3
  44.9 4.4 convolution_bitcast_fusion.3
  49.3 3.6 fusion.18
  54.6 89.1 %all-reduce.6.cloned.1.call-done = bf16[8,256,256]{1,2,0:T(8,128)(2,1)} async-done(((bf16[8,256,256]{1,2,0:T(8,128)(2,1)}), bf16[8,256,256]{1,2,0:T(8,128)(2,1)}) %all-reduce.6.cloned.1.call-update) | async-done | bytes 1048592 | tf_op jit(solution)/shard_map/psum | solution.py:100
  143.7 3.4 fusion.1
  147.1 7.3 %convolution_bitcast_fusion.2 = f32[8,2,256,256]{2,3,0,1:T(8,128)} fusion(f32[8,2,256,256]{2,3,0,1:T(8,128)} %convolution_bitcast_fusion.3, f32[8,256,256]{1,2,0:T(8,128)} %fusion.1, bf16[1,2,256,256]{2,3,0,1:T(8,128)(2,1)S(1)} %copy-done.10, bf16[1,2,256,256]{2,3,0,1:T(8,128)(2,1)S(1)} %copy-done.12, bf16[1,2,256,256]{2,3,1,0:T(8,128)(2,1)S(1)} %copy-done.14, ...), kind=kOutput, calls=%fused_computation.16 | convolution fusion | flops 2151153664 | bytes 11534336 | tf_op jit(solution)/shard_map/...dux,dcxy->...cuy/dot_general | solution.py:38
  154.4 2.8 add_convert_fusion.2
  157.2 1.5 pad_maximum_fusion.1
  159.0 90.1 %all-reduce.12.cloned.1.call-done = (bf16[256,256]{1,0:T(8,128)(2,1)}, bf16[8,2,256,256]{2,3,0,1:T(8,128)(2,1)}) async-done(((bf16[256,256]{1,0:T(8,128)(2,1)}, bf16[8,2,256,256]{2,3,0,1:T(8,128)(2,1)}), (bf16[256,256]{1,0:T(8,128)(2,1)}, bf16[8,2,256,256]{2,3,0,1:T(8,128)(2,1)})) %all-reduce.12.cloned.1.call-update) | async-done | bytes 2228240 | tf_op jit(solution)/shard_map/psum | solution.py:84
  249.1 1.6 reduce_max.14
  251.4 3.3 multiply_add_fusion
  254.7 1.6 subtract_convert_fusion.1
  256.3 5.7 convolution_bitcast_fusion.1
  262.0 3.5 fusion.19
  265.6 86.5 %all-reduce.8.cloned.1.call-done = bf16[8,256,256]{1,2,0:T(8,128)(2,1)} async-done(((bf16[8,256,256]{1,2,0:T(8,128)(2,1)}), bf16[8,256,256]{1,2,0:T(8,128)(2,1)}) %all-reduce.8.cloned.1.call-update) | async-done | bytes 1048592 | tf_op jit(solution)/shard_map/psum | solution.py:100
  352.0 3.4 fusion.3
  355.4 7.3 %convolution_bitcast_fusion = f32[8,2,256,256]{2,3,0,1:T(8,128)} fusion(f32[8,2,256,256]{2,3,0,1:T(8,128)} %convolution_bitcast_fusion.1, f32[8,256,256]{1,2,0:T(8,128)} %fusion.3, bf16[1,2,256,256]{2,3,0,1:T(8,128)(2,1)S(1)} %copy-done.10, bf16[1,2,256,256]{2,3,0,1:T(8,128)(2,1)S(1)} %copy-done.12, bf16[1,2,256,256]{2,3,1,0:T(8,128)(2,1)S(1)} %copy-done.15, ...), kind=kOutput, calls=%fused_computation.14 | convolution fusion | flops 2151153664 | bytes 11534336 | tf_op jit(solution)/shard_map/...dux,dcxy->...cuy/dot_general | solution.py:38
  362.7 2.8 add_convert_fusion
  365.5 1.6 pad_maximum_fusion.2
  398.0 58.7 %all-reduce.10.cloned.1.call-done = bf16[8,2,256,256]{2,3,0,1:T(8,128)(2,1)} async-done(((bf16[8,2,256,256]{2,3,0,1:T(8,128)(2,1)}), bf16[8,2,256,256]{2,3,0,1:T(8,128)(2,1)}) %all-reduce.10.cloned.1.call-update) | async-done | bytes 2097168 | tf_op jit(solution)/shard_map/psum | solution.py:105
  456.7 4.0 subtract_multiply_fusion
  460.7 1.9 copy-done
  462.9 8.7 %dynamic_update_slice.24 = f32[2,512,512]{1,2,0:T(8,128)S(1)} dynamic-update-slice(f32[2,512,512]{1,2,0:T(8,128)S(1)} %broadcast_in_dim.2, f32[2,256,256]{1,2,0:T(8,128)S(1)} %slice_bitcast_fusion.7, s32[]{:T(128)} %constant.13.clone.1, s32[]{:T(128)S(6)} %select_n.109, s32[]{:T(128)S(6)} %select_n.110) | dynamic-update-slice | bytes 1048580 | tf_op jit(solution)/shard_map/dynamic_update_slice | solution.py:116
  472.9 7.2 %dynamic_update_slice.25 = f32[2,512,512]{1,2,0:T(8,128)S(1)} dynamic-update-slice(f32[2,512,512]{1,2,0:T(8,128)S(1)} %dynamic_update_slice.24, f32[2,256,256]{1,2,0:T(8,128)S(1)} %fusion.45, s32[]{:T(128)} %constant.13.clone.1, s32[]{:T(128)S(6)} %select_n.111, s32[]{:T(128)S(6)} %select_n.112) | dynamic-update-slice | bytes 1048580 | tf_op jit(solution)/shard_map/dynamic_update_slice | solution.py:116
  481.4 8.8 %dynamic_update_slice.26 = f32[2,512,512]{1,2,0:T(8,128)S(1)} dynamic-update-slice(f32[2,512,512]{1,2,0:T(8,128)S(1)} %dynamic_update_slice.25, f32[2,256,256]{1,2,0:T(8,128)S(1)} %fusion.44, s32[]{:T(128)} %constant.13.clone.1, s32[]{:T(128)S(6)} %select_n.113, s32[]{:T(128)S(6)} %select_n.114) | dynamic-update-slice | bytes 1048580 | tf_op jit(solution)/shard_map/dynamic_update_slice | solution.py:116
  491.4 8.8 %dynamic_update_slice.27 = f32[2,512,512]{1,2,0:T(8,128)S(1)} dynamic-update-slice(f32[2,512,512]{1,2,0:T(8,128)S(1)} %dynamic_update_slice.26, f32[2,256,256]{1,2,0:T(8,128)S(1)} %fusion.43, s32[]{:T(128)} %constant.13.clone.1, s32[]{:T(128)S(6)} %select_n.115, s32[]{:T(128)S(6)} %select_n.116) | dynamic-update-slice | bytes 1048580 | tf_op jit(solution)/shard_map/dynamic_update_slice | solution.py:116
  501.5 10.1 %dynamic_update_slice.28 = f32[2,512,512]{1,2,0:T(8,128)S(1)} dynamic-update-slice(f32[2,512,512]{1,2,0:T(8,128)S(1)} %dynamic_update_slice.27, f32[2,256,256]{1,2,0:T(8,128)S(1)} %fusion.42, s32[]{:T(128)} %constant.13.clone.1, s32[]{:T(128)S(6)} %select_n.117, s32[]{:T(128)S(6)} %select_n.118) | dynamic-update-slice | bytes 1048580 | tf_op jit(solution)/shard_map/dynamic_update_slice | solution.py:116
  512.9 8.7 %dynamic_update_slice.29 = f32[2,512,512]{1,2,0:T(8,128)S(1)} dynamic-update-slice(f32[2,512,512]{1,2,0:T(8,128)S(1)} %dynamic_update_slice.28, f32[2,256,256]{1,2,0:T(8,128)S(1)} %fusion.41, s32[]{:T(128)} %constant.13.clone.1, s32[]{:T(128)S(6)} %select_n.119, s32[]{:T(128)S(6)} %select_n.120) | dynamic-update-slice | bytes 1048580 | tf_op jit(solution)/shard_map/dynamic_update_slice | solution.py:116
  522.8 9.2 %dynamic_update_slice.30 = f32[2,512,512]{1,2,0:T(8,128)S(1)} dynamic-update-slice(f32[2,512,512]{1,2,0:T(8,128)S(1)} %dynamic_update_slice.29, f32[2,256,256]{1,2,0:T(8,128)S(1)} %fusion.40, s32[]{:T(128)} %constant.13.clone.1, s32[]{:T(128)S(6)} %select_n.121, s32[]{:T(128)S(6)} %select_n.122) | dynamic-update-slice | bytes 1048580 | tf_op jit(solution)/shard_map/dynamic_update_slice | solution.py:116
  532.0 2.1 fusion.39
  534.1 8.5 %dynamic_update_slice.31 = f32[2,512,512]{1,2,0:T(8,128)S(1)} dynamic-update-slice(f32[2,512,512]{1,2,0:T(8,128)S(1)} %dynamic_update_slice.30, f32[2,256,256]{1,2,0:T(8,128)} %fusion.39, s32[]{:T(128)} %constant.13.clone.1, s32[]{:T(128)S(6)} %select_n.123, s32[]{:T(128)S(6)} %select_n.124) | dynamic-update-slice | bytes 1048580 | tf_op jit(solution)/shard_map/dynamic_update_slice | solution.py:116
  543.5 1.9 collective-permute-start.1
  545.4 1.7 select_reduce_fusion
  548.8 1.9 collective-permute-start.2
  552.0 5.0 collective-permute-done.2
  557.0 1.9 fusion.38
  558.9 2.1 copy.42
  560.9 2.5 fusion.21
  563.4 2.5 copy.44
  (107 shorter events, 37.5 us)
Async XLA Ops:
  6.5 4.6 copy-start.16
  6.5 137.2 %all-reduce.6.cloned.1.call-start = ((), (), s32[]{:S(2)}) async-start(), calls=%async_computation | async-start | bytes 2097152 | tf_op jit(solution)/shard_map/psum | solution.py:100
  7.8 8.9 %collective-permute-start = (bf16[2,256,512]{2,1,0:T(8,128)(2,1)S(1)}, bf16[2,256,512]{2,1,0:T(8,128)(2,1)S(1)}, u32[]{:S(2)}, u32[]{:S(2)}) collective-permute-start(bf16[2,256,512]{2,1,0:T(8,128)(2,1)S(1)} %convert_element_type.161), channel_id=1, source_target_pairs={{16,0},{32,16},{48,32},{64,48},{80,64},{96,80},{112,96},{17,1},{33... | collective-permute-start | bytes 1572872 | tf_op jit(solution)/shard_map/ppermute | solution.py:18
  11.3 5.6 copy-start.1
  41.9 2.9 copy-start.9
  41.9 2.9 copy-start.10
  41.9 2.9 copy-start.11
  41.9 2.9 copy-start.13
  49.3 3.7 copy-start.8
  52.9 1.0 copy-start.7
  52.9 196.2 %all-reduce.12.cloned.1.call-start = ((), (), s32[]{:S(2)}) async-start(), calls=%async_computation.3 | async-start | bytes 4456448 | tf_op jit(solution)/shard_map/psum | solution.py:84
  54.6 92.5 %copy-start.12 = (bf16[1,2,256,256]{2,3,0,1:T(8,128)(2,1)S(1)}, bf16[1,2,256,256]{2,3,0,1:T(8,128)(2,1)}, u32[]{:S(2)}) copy-start(bf16[1,2,256,256]{2,3,0,1:T(8,128)(2,1)} %get-tuple-element.39) | copy-start | bytes 786436
  54.6 92.5 %copy-start.14 = (bf16[1,2,256,256]{2,3,1,0:T(8,128)(2,1)S(1)}, bf16[1,2,256,256]{2,3,1,0:T(8,128)(2,1)}, u32[]{:S(2)}) copy-start(bf16[1,2,256,256]{2,3,1,0:T(8,128)(2,1)} %get-tuple-element.40) | copy-start | bytes 786436
  147.1 7.3 %copy-start.4 = (f32[256,256]{0,1:T(8,128)S(1)}, f32[256,256]{0,1:T(8,128)}, u32[]{:S(2)}) copy-start(f32[256,256]{0,1:T(8,128)} %copy.29) | copy-start | bytes 786436
  158.8 193.3 %all-reduce.8.cloned.1.call-start = ((), (), s32[]{:S(2)}) async-start(), calls=%async_computation.1 | async-start | bytes 2097152 | tf_op jit(solution)/shard_map/psum | solution.py:100
  265.5 90.0 %copy-start.15 = (bf16[1,2,256,256]{2,3,1,0:T(8,128)(2,1)S(1)}, bf16[1,2,256,256]{2,3,1,0:T(8,128)(2,1)}, u32[]{:S(2)}) copy-start(bf16[1,2,256,256]{2,3,1,0:T(8,128)(2,1)} %get-tuple-element.40) | copy-start | bytes 786436
  265.5 191.2 %all-reduce.10.cloned.1.call-start = ((), (), s32[]{:S(2)}) async-start(), calls=%async_computation.2 | async-start | bytes 4194304 | tf_op jit(solution)/shard_map/psum | solution.py:105
  367.1 89.6 %copy-start.3 = (bf16[8,2,256,256]{2,3,0,1:T(8,128)(2,1)S(1)}, bf16[8,2,256,256]{2,3,0,1:T(8,128)(2,1)}, u32[]{:S(2)}) copy-start(bf16[8,2,256,256]{2,3,0,1:T(8,128)(2,1)} %get-tuple-element.22) | copy-start | bytes 6291460
  460.7 2.0 copy-start
  534.1 16.6 %copy-start.2 = (f32[2,256,512]{2,1,0:T(8,128)S(1)}, f32[2,256,512]{2,1,0:T(8,128)}, u32[]{:S(2)}) copy-start(f32[2,256,512]{2,1,0:T(8,128)} %param.5) | copy-start | bytes 3145732
  543.5 17.5 %collective-permute-start.1 = (bf16[2,256,512]{1,2,0:T(8,128)(2,1)}, bf16[2,256,512]{1,2,0:T(8,128)(2,1)}, u32[]{:S(2)}, u32[]{:S(2)}) collective-permute-start(bf16[2,256,512]{1,2,0:T(8,128)(2,1)} %slice.330), channel_id=1, source_target_pairs={{0,16},{16,32},{32,48},{48,64},{64,80},{80,96},{96,112},{1,17},{17... | collective-permute-start | bytes 1572872 | tf_op jit(solution)/shard_map/ppermute | solution.py:18
  547.1 1.0 copy-start.6
  548.8 8.2 %collective-permute-start.2 = (bf16[256,512]{1,0:T(8,128)(2,1)}, bf16[256,512]{1,0:T(8,128)(2,1)S(1)}, u32[]{:S(2)}, u32[]{:S(2)}) collective-permute-start(bf16[256,512]{1,0:T(8,128)(2,1)} %slice.331), channel_id=1, source_target_pairs={{0,16},{16,32},{32,48},{48,64},{64,80},{80,96},{96,112},{1,17},{17... | collective-permute-start | bytes 786440 | tf_op jit(solution)/shard_map/ppermute | solution.py:18
  552.0 8.9 %copy-start.5 = (f32[2,256,512]{1,2,0:T(8,128)S(1)}, f32[2,256,512]{1,2,0:T(8,128)}, u32[]{:S(2)}) copy-start(f32[2,256,512]{1,2,0:T(8,128)} %copy.43) | copy-start | bytes 3145732
Sparse Core Ops, SparseCore 0:
  53.0 90.6 all-reduce.5
  158.9 90.1 all-reduce.11
  265.6 86.3 all-reduce.7
  367.2 89.4 all-reduce.9
where the time goes:
time: 574 us; the launch traced here: 572 us
  waiting for transfers between devices  331 us (58%)
  local copies, waits for them, and re-layouts  109 us (19%)
  other arithmetic  57.2 us (10%)
  between operations  44.2 us (8%)
  matrix products  24.6 us (4%)
  starting transfers between devices  6.3 us (1%)
    psum x2, waiting for transfers between devices, shards(): lax.psum(own_intensity.astype(jnp.bfloat16), 'mode').astype(jnp.float32)  176 us
    psum x1, waiting for transfers between devices, shards(): lax.psum(jnp.sum(probe_modes[:, 0] ** 2 + probe_modes[:, 1] ** 2, axis=0)...  90.1 us
    dynamic_update_slice x8, local copies, waits for them, and re-layouts, shards(): lax.dynamic_update_slice(summed, piece, (jnp.int32(0), row_start, col_sta...  70 us
    psum x1, waiting for transfers between devices, shards(): lax.psum(mode_term.astype(jnp.bfloat16), 'mode').astype(jnp.float32)  58.7 us
    gather x40, local copies, waits for them, and re-layouts  24.8 us
    dot_general x4, matrix products, transform(): jnp.einsum('...dux,dcxy->...cuy', halfway, second_table, preferred_elemen...  24.6 us
  transfers between devices with their start and end apart: 7, of which 6 were waited for; matrix products, arithmetic and copies ran while one was open for 3% of the time, Pallas kernels for 0%

commit v1 on v0

v1 whole, which is shorter than its diff:
```python
import math

import numpy as np
import ml_dtypes
import jax
import jax.numpy as jnp
from jax import lax
from jax.experimental import pallas as pl
from jax.experimental.pallas import tpu as pltpu
from jax.sharding import PartitionSpec as P

PATCH = 256
HALF = 128
PASSES = 2
STEP_SIZE = 0.9
SLAB = 16
MESH = pl.DeviceIdType.MESH
BF16 = jnp.bfloat16
F32 = jnp.float32

ORDER = ((0, 0), (1, 0), (0, 1), (0, 3), (1, 1), (1, 3), (0, 2), (1, 2))


def make_tables():
    q = np.arange(HALF)
    tables = []
    for s in range(2):
        a = 2 * np.arange(HALF) + s
        angle = (q[:, None] * a[None, :] % PATCH).astype(np.float32) * np.float32(2.0 * math.pi / PATCH)
        factor = np.float32(1.0 / math.sqrt(PATCH))
        real = (np.cos(angle) * factor).astype(ml_dtypes.bfloat16)
        imag = (-np.sin(angle) * factor).astype(ml_dtypes.bfloat16)
        tables.append(np.block([[real, -imag], [imag, real]]))
    tables = np.stack(tables)
    return np.stack([tables, tables.transpose(0, 2, 1)])


def mm(a, b):
    return jnp.dot(a, b, preferred_element_type=F32)


def natural(position):
    return jnp.where(position < HALF, 2 * position, 2 * position - (PATCH - 1))


def kernel(
    obj_hbm, probe_hbm, pat_hbm, tab_hbm, offs_ref, counts_ref, out_hbm,
    probe, strip, strip_b, ext, pat, tab, info, modes, half, far, init, cur,
    inten, ratio, upd, power, inten_b, upd_b, last_b, power_b, inten_in, upd_in, last_in, power_in,
    place_r, place_c, canvas, slabs, spill, spill_in, ring_y, ring_z,
    local_sem, gather_send, gather_recv, strip_sem, info_sem, patch_sem, pat_sem,
    pair_send, pair_recv, slab_send, slab_recv, spill_sem, ring_send, ring_recv,
):
    t = lax.axis_index("tile")
    j = lax.axis_index("mode")
    x, z = t // 2, j // 4
    c, y = t - 2 * x, j - 4 * z
    group = z // 2
    owner = c == group
    s_tile = 2 * x + group
    slot = j - 8 * group
    partner = 2 * x + (1 - c)
    up_tile = (t + 1) % 8
    down_tile = (t + 7) % 8

    load_probe = pltpu.make_async_copy(probe_hbm.at[0], probe, local_sem.at[0])
    load_strip = pltpu.make_async_copy(obj_hbm, strip, local_sem.at[1])
    load_tab = pltpu.make_async_copy(tab_hbm, tab, local_sem.at[2])
    load_pat = pltpu.make_async_copy(pat_hbm.at[slot], pat, local_sem.at[3])
    @pl.when(owner)
    def _():
        load_probe.start()
        load_pat.start()

    load_strip.start()
    load_tab.start()

    barrier = pltpu.get_barrier_semaphore()

    def greet(tile, mode):
        pl.semaphore_signal(barrier, inc=1, device_id=(tile, mode), device_id_type=MESH)

    for k in range(1, 16):
        greet(t, (j + k) % 16)
    greet(partner, j)
    across = jnp.where(c == 1, up_tile, down_tile)
    greet(across, j)
    for k in range(8):
        greet(partner, 8 * c + k)

    lane = lax.broadcasted_iota(jnp.int32, (8, HALF), 1)
    live = (lax.broadcasted_iota(jnp.int32, (8, HALF), 0) < counts_ref[0]).astype(jnp.int32)
    offs = offs_ref[...]
    info[0] = jnp.where(lane == 0, offs[:, 0:1], jnp.where(lane == 1, offs[:, 1:2], live))

    pl.semaphore_wait(barrier, 15 + 2 + jnp.where(owner, 0, 16))

    def to(src, dst, send, recv, tile, mode):
        return pltpu.make_async_remote_copy(
            src_ref=src, dst_ref=dst, send_sem=send, recv_sem=recv,
            device_id=(tile, mode), device_id_type=MESH,
        )

    info_pair = to(info.at[0], info.at[1], info_sem.at[0], info_sem.at[1], partner, j)
    info_next = to(info.at[0], info.at[2], info_sem.at[2], info_sem.at[3], up_tile, j)
    info_pair.start()

    @pl.when(c == 1)
    def _():
        info_next.start()

    def block(m, s, h):
        return modes.at[m, s, pl.ds(h * HALF, HALF), :]

    def mode_slot(row, home, dy):
        d = (row - 2 * c + 4) % 4
        nearer = 2 * c + jnp.where((d == 1) | (d == 2), 1, 0)
        return jnp.where(home == nearer, ORDER.index((0, dy)), ORDER.index((1, dy)))

    def relay(k, s, h, home, dy, step_z, step_y):
        row = (z + step_z + 4) % 4
        there = mode_slot(row, home, (dy + step_y) % 4)
        to(
            block(k, s, h), block(there, s, h), gather_send, gather_recv.at[there, s, h],
            t, row * 4 + (y + step_y + 4) % 4,
        ).start()

    def take(k):
        which, dy = ORDER[k]
        d = (z - 2 * c + 4) % 4
        nearer = jnp.where((d == 1) | (d == 2), 1, 0)
        home = 2 * c + (nearer if which == 0 else 1 - nearer)
        dz = (z - home + 4) % 4
        for h in range(2):
            for s in range(2):
                def wait():
                    to(
                        block(k, s, h), block(k, s, h), gather_send, gather_recv.at[k, s, h], t, j
                    ).wait_recv()

                if k == 0:
                    pl.when(dz != 0)(wait)
                else:
                    wait()
                steps = []
                if dy == 0 or (dy == 1 and h == 0):
                    steps.append(1)
                if dy == 0 or (dy == 3 and h == 1):
                    steps.append(-1)

                def along_y():
                    for step in steps:
                        relay(k, s, h, home, dy, 0, step)

                if steps and s == 0:
                    pl.when(dz == 0)(along_y)
                elif steps:
                    along_y()
                if s == 0 or dy == 0:
                    up = (dz == 0) | (dz == 1) if h == 0 else dz == 0
                    down = (dz == 0) | (dz == 3) if h == 1 else dz == 0
                    for step, wanted in ((1, up), (-1, down)):
                        @pl.when(wanted)
                        def _():
                            relay(k, s, h, home, dy, step, 0)

    @pl.when(owner)
    def _():
        load_probe.wait()
        rows = lax.broadcasted_iota(jnp.int32, (PATCH, PATCH), 0)
        cols = lax.broadcasted_iota(jnp.int32, (PATCH, PATCH), 1)
        sort_r = jnp.where(cols == natural(rows), 1.0, 0.0).astype(BF16)
        sort_c = jnp.where(rows == natural(cols), 1.0, 0.0).astype(BF16)
        for ri in range(2):
            plane = mm(sort_r, probe[ri].astype(BF16)).astype(BF16)
            plane = mm(plane, sort_c).astype(BF16)
            for s in range(2):
                modes[0, s, ri * HALF:(ri + 1) * HALF, :] = plane[s * HALF:(s + 1) * HALF]
        take(0)

    send_strip = to(
        strip_b, ext.at[:, pl.ds(PATCH, PATCH), :], strip_sem.at[0], strip_sem.at[1], down_tile, j
    )
    pat_pair = to(pat_hbm.at[slot], pat, pat_sem.at[0], pat_sem.at[1], partner, j)
    load_strip.wait()

    @pl.when(jnp.logical_not(owner))
    def _():
        strip_b[...] = strip[...].astype(BF16)
        send_strip.start()

    @pl.when(owner)
    def _():
        pat_pair.start()
        high = strip[...].astype(BF16)
        ext[:, 0:PATCH, :] = high
        strip_b[...] = (strip[...] - high.astype(F32)).astype(BF16)

    @pl.when(jnp.logical_not(owner))
    def _():
        take(0)

    for k in range(1, 4):
        take(k)

    load_tab.wait()
    info_pair.wait_recv()

    @pl.when(owner)
    def _():
        info[3] = info[0]

    @pl.when(jnp.logical_not(owner))
    def _():
        info[3] = info[1]

    row = info[3, pl.ds(slot, 1), :]
    first_row, first_col, alive = row[:, 0:1], row[:, 1:2], row[:, 2:3]
    rows = lax.broadcasted_iota(jnp.int32, (PATCH, PATCH), 0)
    cols = lax.broadcasted_iota(jnp.int32, (PATCH, PATCH), 1)

    def wrapped(at):
        return jnp.where(at >= PATCH, at - PATCH, at)

    place_r[...] = jnp.where((rows == wrapped(first_row + natural(cols))) & (alive > 0), 1.0, 0.0).astype(BF16)
    place_c[...] = jnp.where(cols == wrapped(first_col + natural(rows)), 1.0, 0.0).astype(BF16)

    send_patch = to(init, init, patch_sem.at[0], patch_sem.at[1], partner, j)

    @pl.when(owner)
    def _():
        send_strip.wait_recv()
        inside = jnp.where(t == 7, PATCH, 2 * PATCH)
        rows = lax.broadcasted_iota(jnp.int32, (PATCH, 2 * PATCH), 0)
        cols = lax.broadcasted_iota(jnp.int32, (PATCH, 2 * PATCH), 1)
        cut_r = jnp.where((cols == first_row + natural(rows)) & (cols < inside), 1.0, 0.0).astype(BF16)
        rows2 = lax.broadcasted_iota(jnp.int32, (2 * PATCH, PATCH), 0)
        cols2 = lax.broadcasted_iota(jnp.int32, (2 * PATCH, PATCH), 1)
        cut_c = jnp.where(rows2 == first_col + natural(cols2), 1.0, 0.0).astype(BF16)
        for ri in range(2):
            high = mm(cut_r, ext[ri]).astype(BF16)
            low = mm(cut_r[:, 0:PATCH], strip_b[ri]).astype(BF16)
            piece = mm(high, cut_c) + mm(low, cut_c)
            for s in range(2):
                init[s, ri * HALF:(ri + 1) * HALF, :] = piece[s * HALF:(s + 1) * HALF]
        send_patch.start()

    for k in range(4, 6):
        take(k)

    @pl.when(owner)
    def _():
        load_pat.wait()
        pat_pair.wait_send()
        send_patch.wait_send()

    @pl.when(jnp.logical_not(owner))
    def _():
        pat_pair.wait_recv()
        send_patch.wait_recv()
        send_strip.wait_send()

    def far_rows(m, b):
        return pl.ds((2 * m + b) * PATCH, PATCH)

    def exit_and_left(m, field, with_power):
        ends = []
        for s in range(2):
            pr = modes[m, s, 0:HALF, :].astype(F32)
            pi = modes[m, s, HALF:PATCH, :].astype(F32)
            cr = field[s, 0:HALF, :]
            ci = field[s, HALF:PATCH, :]
            wave = jnp.concatenate(
                [(pr * cr - pi * ci).astype(BF16), (pr * ci + pi * cr).astype(BF16)], axis=0
            )
            if with_power:
                power[s] += pr * pr + pi * pi
            ends.append(mm(tab[0, s], wave))
        for b, part in enumerate((ends[0] + ends[1], ends[0] - ends[1])):
            part = part.astype(BF16)
            for s in range(2):
                for ri in range(2):
                    half[m, s, b * HALF:(b + 1) * HALF, ri * HALF:(ri + 1) * HALF] = part[
                        ri * HALF:(ri + 1) * HALF, s * HALF:(s + 1) * HALF
                    ]

    def right_and_power(first):
        sums = [0.0, 0.0]
        for m in (first, first + 1):
            even = mm(half[m, 0], tab[1, 0])
            odd = mm(half[m, 1], tab[1, 1])
            for b, part in enumerate((even + odd, even - odd)):
                far[far_rows(m, b), :] = part
                re, im = part[:, 0:HALF], part[:, HALF:PATCH]
                sums[b] += re * re + im * im
        for b in range(2):
            inten[b] = sums[b] if first == 0 else inten[b] + sums[b]

    def change_and_right(m):
        ra, rb = ratio[0], ratio[1]
        ya = far[far_rows(m, 0), :] * jnp.concatenate([ra, ra], axis=1)
        yb = far[far_rows(m, 1), :] * jnp.concatenate([rb, rb], axis=1)
        for s, part in enumerate(((ya + yb).astype(BF16), (ya - yb).astype(BF16))):
            near = mm(part, tab[0, s])
            lo, hi = near[0:HALF], near[HALF:PATCH]
            for b, mixed in enumerate((lo + hi, lo - hi)):
                mixed = mixed.astype(BF16)
                for ri in range(2):
                    half[m, b, ri * HALF:(ri + 1) * HALF, s * HALF:(s + 1) * HALF] = mixed[
                        :, ri * HALF:(ri + 1) * HALF
                    ]

    def left_and_update(first):
        for s in range(2):
            re = im = 0.0
            for m in (first, first + 1):
                near = mm(tab[1, s], half[m, s])
                nr, ni = near[0:HALF], near[HALF:PATCH]
                pr = modes[m, s, 0:HALF, :].astype(F32)
                pi = modes[m, s, HALF:PATCH, :].astype(F32)
                re += pr * nr + pi * ni
                im += pr * ni - pi * nr
            if first == 0:
                upd[s, 0:HALF, :] = re
                upd[s, HALF:PATCH, :] = im
            else:
                upd[s, 0:HALF, :] += re
                upd[s, HALF:PATCH, :] += im

    def swap(src, dst, which):
        copy = to(src, dst, pair_send.at[which], pair_recv.at[which], partner, j)
        copy.start()
        return copy

    power[...] = jnp.zeros_like(power)
    for repeat in range(PASSES):
        last = repeat == PASSES - 1
        if repeat == 0:
            for k in range(4):
                exit_and_left(k, init, True)
            take(6)
            for k in range(4, 6):
                exit_and_left(k, init, True)
            take(7)
            for k in range(6, 8):
                exit_and_left(k, init, True)
        else:
            for k in range(8):
                exit_and_left(k, cur, False)
        for k in range(0, 8, 2):
            right_and_power(k)
        inten_b[repeat] = inten[...].astype(BF16)
        copy = swap(inten_b.at[repeat], inten_in.at[repeat], 3 * repeat)
        if repeat == 0:
            power_b[...] = power[...].astype(BF16)
            power_copy = swap(power_b, power_in, 1)
        copy.wait()
        for b in range(2):
            total = inten[b] + inten_in[repeat, b].astype(F32)
            measured = pat[:, b * HALF:(b + 1) * HALF].astype(F32)
            ratio[b] = jnp.sqrt(measured / jnp.maximum(total, 1.0)) - 1.0

        for k in range(8):
            change_and_right(k)
        for k in range(0, 8, 2):
            left_and_update(k)
        if repeat == 0:
            power_copy.wait()
            whole = power[...] + power_in[...].astype(F32)
            whole = jnp.maximum(whole[0], whole[1])
            highest = jnp.max(jnp.max(whole, axis=0, keepdims=True), axis=1, keepdims=True)
            scale = STEP_SIZE / highest
        if not last:
            upd_b[...] = upd[...].astype(BF16)
            copy = swap(upd_b, upd_in, 2)
            copy.wait()
            for s in range(2):
                cur[s] = init[s] + scale * (upd[s] + upd_in[s].astype(F32))
        else:
            mine = pl.ds(pl.multiple_of(c * HALF, HALF), HALF)
            other = pl.ds(pl.multiple_of((1 - c) * HALF, HALF), HALF)
            last_b[...] = upd[:, other, :].astype(BF16)
            copy = swap(last_b, last_in, 4)
            copy.wait()
            moved = []
            for s in range(2):
                change = cur[s, mine, :] - init[s, mine, :]
                change += scale * (upd[s, mine, :] + last_in[s].astype(F32))
                moved.append(change.astype(BF16))
            moved = jnp.concatenate(moved, axis=0)

    placed = mm(place_r[...], moved).astype(BF16)
    canvas[...] = mm(placed, place_c[...]).astype(BF16)

    for step in range(16):
        mode = (j + step) % 16
        src = canvas.at[pl.ds(pl.multiple_of(mode * SLAB, SLAB), SLAB), :]
        dst = slabs.at[c * 8 + slot]
        if step == 0:
            @pl.when(owner)
            def _():
                pltpu.make_async_copy(src, dst, slab_recv).start()

            @pl.when(jnp.logical_not(owner))
            def _():
                to(src, dst, slab_send, slab_recv, s_tile, mode).start()
        else:
            to(src, dst, slab_send, slab_recv, s_tile, mode).start()

    @pl.when(c == 0)
    def _():
        info_next.wait_recv()
        info[4] = info[2]

    @pl.when(c == 1)
    def _():
        info[4] = info[1]

    at_row = lax.broadcasted_iota(jnp.int32, (SLAB, 2 * PATCH), 0) + j * SLAB
    at_col = lax.broadcasted_iota(jnp.int32, (SLAB, 2 * PATCH), 1)
    from_above = jnp.where(t > 0, 1.0, 0.0)
    cover = jnp.zeros((SLAB, 2 * PATCH), F32)
    for k in range(2):
        here = info[4 * k]
        part = jnp.zeros((SLAB, 2 * PATCH), F32)
        for i in range(8):
            dr = at_row + k * PATCH - here[i:i + 1, 0:1]
            dc = at_col - here[i:i + 1, 1:2]
            inside = (dr >= 0) & (dr < PATCH) & (dc >= 0) & (dc < PATCH) & (here[i:i + 1, 2:3] > 0)
            part += jnp.where(inside, 1.0, 0.0)
        cover += part if k == 0 else part * from_above
    share = 1.0 / jnp.maximum(cover, 1.0)

    pltpu.make_async_copy(slabs, slabs, slab_recv).wait()
    at_row = lax.broadcasted_iota(jnp.int32, (SLAB, PATCH), 0) + j * SLAB
    at_col = lax.broadcasted_iota(jnp.int32, (SLAB, PATCH), 1)
    own = []
    for ri in range(2):
        parts = [jnp.zeros((SLAB, PATCH), F32) for _ in range(4)]
        for i in range(8):
            value = slabs[ri * 8 + i].astype(F32)
            in_strip = at_row >= info[0, i:i + 1, 0:1]
            in_left = at_col >= info[0, i:i + 1, 1:2]
            left = jnp.where(in_left, value, 0.0)
            right = value - left
            left_own = jnp.where(in_strip, left, 0.0)
            right_own = jnp.where(in_strip, right, 0.0)
            for p, term in enumerate((left_own, right_own, left - left_own, right - right_own)):
                parts[p] += term
        own.append(jnp.concatenate(parts[0:2], axis=1))
        spill[ri] = jnp.concatenate(parts[2:4], axis=1).astype(BF16)

    spill_copy = to(spill, spill_in, spill_sem.at[0], spill_sem.at[1], up_tile, j)
    spill_copy.start()
    spill_copy.wait()
    ring_y[y] = ((own[0] + spill_in[0].astype(F32) * from_above) * share).astype(BF16)
    ring_z[z] = ((own[1] + spill_in[1].astype(F32) * from_above) * share).astype(BF16)

    for k in range(1, 4):
        to(ring_y.at[y], ring_y.at[y], ring_send.at[0], ring_recv.at[0], t, 4 * z + (y + k) % 4).start()
        to(ring_z.at[z], ring_z.at[z], ring_send.at[1], ring_recv.at[1], t, 4 * ((z + k) % 4) + y).start()
    keep = (
        pltpu.make_async_copy(ring_y, out_hbm.at[0, z], local_sem.at[4]),
        pltpu.make_async_copy(ring_z, out_hbm.at[1, :, y], local_sem.at[5]),
    )
    three = ring_y.at[pl.ds(0, 3)]
    for p in range(2):
        pltpu.make_async_copy(three, three, ring_recv.at[p]).wait()
        for k in range(1, 4):
            if p == 0:
                to(ring_y, out_hbm.at[0, z], ring_send.at[2], ring_recv.at[2], t, 4 * ((z + k) % 4) + y).start()
            else:
                to(ring_z, out_hbm.at[1, :, y], ring_send.at[3], ring_recv.at[3], t, 4 * z + (y + k) % 4).start()
        keep[p].start()

    info_pair.wait_send()

    @pl.when(c == 1)
    def _():
        info_next.wait_send()

    for here, count in ((owner, 43), (jnp.logical_not(owner), 17)):
        @pl.when(here)
        def _():
            rows = far.at[pl.ds(0, count * 64), :]
            pltpu.make_async_copy(rows, rows, gather_send).wait()

    for here, count in ((owner, 15), (jnp.logical_not(owner), 16)):
        @pl.when(here)
        def _():
            rows = slabs.at[pl.ds(0, count)]
            pltpu.make_async_copy(rows, rows, slab_send).wait()

    rings = strip.at[0, pl.ds(0, 96), :]
    for p in range(2):
        pltpu.make_async_copy(three, three, ring_send.at[p]).wait()
        pltpu.make_async_copy(rings, rings, ring_send.at[2 + p]).wait()
        pltpu.make_async_copy(rings, rings, ring_recv.at[2 + p]).wait()
        keep[p].wait()


def shards(object_field, probe_modes, patterns, offsets, counts):
    tables = jnp.asarray(make_tables())
    any_space = pl.BlockSpec(memory_space=pl.ANY)
    vmem = pltpu.VMEM
    dma = pltpu.SemaphoreType.DMA
    change = pl.pallas_call(
        kernel,
        out_shape=jax.ShapeDtypeStruct((2, 4, 4, SLAB, 2 * PATCH), BF16),
        in_specs=[
            any_space, any_space, any_space, any_space,
            pl.BlockSpec(memory_space=vmem),
            pl.BlockSpec(memory_space=pltpu.SMEM),
        ],
        out_specs=any_space,
        scratch_shapes=[
            vmem((2, PATCH, PATCH), F32),
            vmem((2, PATCH, 2 * PATCH), F32),
            vmem((2, PATCH, 2 * PATCH), BF16),
            vmem((2, 2 * PATCH, 2 * PATCH), BF16),
            vmem((PATCH, PATCH), BF16),
            vmem((2, 2, PATCH, PATCH), BF16),
            vmem((5, 8, HALF), jnp.int32),
            vmem((8, 2, PATCH, PATCH), BF16),
            vmem((8, 2, PATCH, PATCH), BF16),
            vmem((16 * PATCH, PATCH), F32),
            vmem((2, PATCH, PATCH), F32),
            vmem((2, PATCH, PATCH), F32),
            vmem((2, PATCH, HALF), F32),
            vmem((2, PATCH, HALF), F32),
            vmem((2, PATCH, PATCH), F32),
            vmem((2, HALF, PATCH), F32),
            vmem((PASSES, 2, PATCH, HALF), BF16),
            vmem((2, PATCH, PATCH), BF16),
            vmem((2, HALF, PATCH), BF16),
            vmem((2, HALF, PATCH), BF16),
            vmem((PASSES, 2, PATCH, HALF), BF16),
            vmem((2, PATCH, PATCH), BF16),
            vmem((2, HALF, PATCH), BF16),
            vmem((2, HALF, PATCH), BF16),
            vmem((PATCH, PATCH), BF16),
            vmem((PATCH, PATCH), BF16),
            vmem((PATCH, PATCH), BF16),
            vmem((16, SLAB, PATCH), BF16),
            vmem((2, SLAB, 2 * PATCH), BF16),
            vmem((2, SLAB, 2 * PATCH), BF16),
            vmem((4, SLAB, 2 * PATCH), BF16),
            vmem((4, SLAB, 2 * PATCH), BF16),
            dma((6,)), dma, dma((8, 2, 2)), dma((2,)), dma((4,)), dma((2,)), dma((2,)),
            dma((5,)), dma((5,)), dma, dma, dma((2,)), dma((4,)), dma((4,)),
        ],
        compiler_params=pltpu.CompilerParams(
            collective_id=0, has_side_effects=True, vmem_limit_bytes=60 * 1024 * 1024
        ),
        cost_estimate=pl.CostEstimate(flops=6 * 10**9, bytes_accessed=8 * 2**20, transcendentals=131072),
    )(object_field, probe_modes, patterns, tables, offsets, counts)
    return object_field + change.reshape(object_field.shape).astype(F32)


def solution(mesh):
    return jax.shard_map(
        shards,
        mesh=mesh,
        in_specs=(
            P(None, "tile", None),
            P("mode", None, None, None),
            P("tile", None, None),
            P("tile", None),
            P("tile"),
        ),
        out_specs=P(None, "tile", None),
        check_vma=False,
    )
```

time: 574 us -> 64.5 us (0.11)
  the two profiles are of different devices: /device:TPU:6 before, /device:TPU:0 now
where the time goes in v1:
time: 64.5 us; the launch traced here: 64.3 us
  Pallas kernels  60.7 us (94%)
  other arithmetic  2.19 us (3%)
  local copies, waits for them, and re-layouts  0.69 us (1%)
  between operations  0.68 us (1%)
    pallas_call x1, Pallas kernels, shards(): pl.pallas_call(kernel, out_shape=jax.ShapeDtypeStruct((2, 4, 4, SLAB, 2 *...  60.7 us
    add x1, other arithmetic, shards(): return object_field + change.reshape(object_field.shape).astype(F32)  2.19 us

profile of v1, /device:TPU:0, one launch (start us, length us, event | category | flops | bytes accessed | tf_op | source)
XLA Modules:
  0.0 64.3 jit_solution(13567162040532390852)
XLA Ops:
  0.0 0.0 copy-start.1
  0.7 0.0 copy-done.1
  0.7 0.7 %copy.7.offs_ref = s32[8,2]{1,0:T(8,128)} copy(s32[8,2]{0,1:T(2,128)S(1)} %copy-done.1) | data formatting | bytes 128 | tf_op args[3]
  1.4 0.0 copy-start
  1.4 60.7 %shard_map.64 = bf16[2,4,4,16,512]{4,3,2,1,0:T(8,128)(2,1)} custom-call(f32[2,256,512]{2,1,0:T(8,128)} %obj_hbm.1, f32[1,2,256,256]{3,2,1,0:T(8,128)} %probe_hbm.1, bf16[8,256,256]{2,1,0:T(8,128)(2,1)} %pat_hbm.1, bf16[2,2,256,256]{3,2,1,0:T(8,128)(2,1)} %constant.2.clone.tab_hbm, s32[8,2]{1,0:T(8,128)} %copy.7.offs_ref, s32[1]{0:T(128)S(6)} %copy.8.counts_ref), custom_call_target="tpu_custom_call" | custom-call | flops 6000000000 | bytes 8388608 | tf_op jit(solution)/shard_map/pallas_call | solution.py:507
  62.1 0.0 copy-done
  62.1 2.2 %convert_add_fusion = f32[2,256,512]{2,1,0:T(8,128)} fusion(f32[2,256,512]{2,1,0:T(8,128)S(1)} %copy-done, bf16[2,4,4,16,512]{4,3,2,1,0:T(8,128)(2,1)} %shard_map.64), kind=kLoop, calls=%fused_computation | loop fusion | flops 524288 | bytes 2621440 | tf_op jit(solution)/shard_map/add | solution.py:557
Async XLA Ops:
  0.0 0.7 %copy-start.1 = (s32[8,2]{0,1:T(2,128)S(1)}, s32[8,2]{0,1:T(2,128)}, u32[]{:S(2)}) copy-start(s32[8,2]{0,1:T(2,128)} %param.9) | copy-start | bytes 196
  1.4 60.8 %copy-start = (f32[2,256,512]{2,1,0:T(8,128)S(1)}, f32[2,256,512]{2,1,0:T(8,128)}, u32[]{:S(2)}) copy-start(f32[2,256,512]{2,1,0:T(8,128)} %obj_hbm.1) | copy-start | bytes 3145732

commit v2 on v1

--- a/solution.py
+++ b/solution.py
@@ -19,6 +19,9 @@
 F32 = jnp.float32
 
 ORDER = ((0, 0), (1, 0), (0, 1), (0, 3), (1, 1), (1, 3), (0, 2), (1, 2))
+FAR_FIRST = sorted(
+    ((dz, dy) for dz in range(4) for dy in range(4)), key=lambda d: -min(d[0], 4 - d[0]) - min(d[1], 4 - d[1])
+)
 
 
 def make_tables():
@@ -47,9 +50,9 @@
     obj_hbm, probe_hbm, pat_hbm, tab_hbm, offs_ref, counts_ref, out_hbm,
     probe, strip, strip_b, ext, pat, tab, info, modes, half, far, init, cur,
     inten, ratio, upd, power, inten_b, upd_b, last_b, power_b, inten_in, upd_in, last_in, power_in,
-    place_r, place_c, canvas, slabs, spill, spill_in, ring_y, ring_z,
+    place_r, place_c, canvas, slabs, spill, spill_in, own, quot,
     local_sem, gather_send, gather_recv, strip_sem, info_sem, patch_sem, pat_sem,
-    pair_send, pair_recv, slab_send, slab_recv, spill_sem, ring_send, ring_recv,
+    pair_send, pair_recv, slab_send, slab_recv, spill_sem, quot_send, quot_recv,
 ):
     t = lax.axis_index("tile")
     j = lax.axis_index("mode")
@@ -60,8 +63,7 @@
     s_tile = 2 * x + group
     slot = j - 8 * group
     partner = 2 * x + (1 - c)
-    up_tile = (t + 1) % 8
-    down_tile = (t + 7) % 8
+    up_tile, down_tile = t + 1, t - 1
 
     load_probe = pltpu.make_async_copy(probe_hbm.at[0], probe, local_sem.at[0])
     load_strip = pltpu.make_async_copy(obj_hbm, strip, local_sem.at[1])
@@ -83,17 +85,43 @@
     for k in range(1, 16):
         greet(t, (j + k) % 16)
     greet(partner, j)
-    across = jnp.where(c == 1, up_tile, down_tile)
-    greet(across, j)
+    has_up, has_down = t < 7, t > 0
+    to_next_x = (c == 1) & has_up
+    to_prev_x = (c == 0) & has_down
+
+    @pl.when(to_next_x)
+    def _():
+        greet(up_tile, j)
+
+    @pl.when(to_prev_x)
+    def _():
+        greet(down_tile, j)
+        for k in range(8):
+            for core in range(2):
+                greet(2 * x - 2 + core, 8 + k)
+
     for k in range(8):
         greet(partner, 8 * c + k)
 
     lane = lax.broadcasted_iota(jnp.int32, (8, HALF), 1)
     live = (lax.broadcasted_iota(jnp.int32, (8, HALF), 0) < counts_ref[0]).astype(jnp.int32)
-    offs = offs_ref[...]
-    info[0] = jnp.where(lane == 0, offs[:, 0:1], jnp.where(lane == 1, offs[:, 1:2], live))
-
-    pl.semaphore_wait(barrier, 15 + 2 + jnp.where(owner, 0, 16))
+    place = jnp.where(lane == 2, live, 0)
+    line = lax.broadcasted_iota(jnp.int32, (8, HALF), 0)
+    for i in range(8):
+        for p in range(2):
+            place = jnp.where((line == i) & (lane == p), offs_ref[p, i], place)
+    info[0] = place
+
+    @pl.when(jnp.logical_not(has_down))
+    def _():
+        info[2] = jnp.zeros((8, HALF), jnp.int32)
+
+
+    far_slabs = (group == 1) & (x < 3)
+    across = to_next_x | to_prev_x
+    pl.semaphore_wait(
+        barrier, 16 + jnp.where(across, 1, 0) + jnp.where(owner, 0, 16) + jnp.where(far_slabs, 16, 0)
+    )
 
     def to(src, dst, send, recv, tile, mode):
         return pltpu.make_async_remote_copy(
@@ -105,7 +133,7 @@
     info_next = to(info.at[0], info.at[2], info_sem.at[2], info_sem.at[3], up_tile, j)
     info_pair.start()
 
-    @pl.when(c == 1)
+    @pl.when(to_next_x)
     def _():
         info_next.start()
 
@@ -142,27 +170,36 @@
                     pl.when(dz != 0)(wait)
                 else:
                     wait()
-                steps = []
-                if dy == 0 or (dy == 1 and h == 0):
-                    steps.append(1)
-                if dy == 0 or (dy == 3 and h == 1):
-                    steps.append(-1)
-
-                def along_y():
-                    for step in steps:
+                if s == 0 and dy == 0:
+                    @pl.when(dz == 0)
+                    def _():
+                        for step in (2, 1, -1):
+                            relay(k, s, h, home, dy, 0, step)
+
+                if s == 1 and dy == 0:
+                    @pl.when(dz == 2)
+                    def _():
+                        relay(k, s, h, home, dy, 0, 2)
+
+                    for step in (1, -1):
                         relay(k, s, h, home, dy, 0, step)
-
-                if steps and s == 0:
-                    pl.when(dz == 0)(along_y)
-                elif steps:
-                    along_y()
+                if s == 1 and (dy, h) in ((1, 0), (3, 1)):
+                    @pl.when(dz != 2)
+                    def _():
+                        relay(k, s, h, home, dy, 0, 2 - dy)
+
                 if s == 0 or dy == 0:
-                    up = (dz == 0) | (dz == 1) if h == 0 else dz == 0
-                    down = (dz == 0) | (dz == 3) if h == 1 else dz == 0
-                    for step, wanted in ((1, up), (-1, down)):
-                        @pl.when(wanted)
-                        def _():
-                            relay(k, s, h, home, dy, step, 0)
+                    @pl.when(dz == 0)
+                    def _():
+                        if s == 1 or dy == 2:
+                            relay(k, s, h, home, dy, 2, 0)
+                        relay(k, s, h, home, dy, 1, 0)
+                        relay(k, s, h, home, dy, -1, 0)
+
+                if s == 0 and dy != 2:
+                    @pl.when(dz == (1 if h == 0 else 3))
+                    def _():
+                        relay(k, s, h, home, dy, 1 if h == 0 else -1, 0)
 
     @pl.when(owner)
     def _():
@@ -184,10 +221,16 @@
     pat_pair = to(pat_hbm.at[slot], pat, pat_sem.at[0], pat_sem.at[1], partner, j)
     load_strip.wait()
 
-    @pl.when(jnp.logical_not(owner))
+    sends_strip = jnp.logical_not(owner) & has_down
+
+    @pl.when(sends_strip)
     def _():
         strip_b[...] = strip[...].astype(BF16)
         send_strip.start()
+
+    @pl.when(t == 7)
+    def _():
+        ext[:, PATCH:2 * PATCH, :] = jnp.zeros((2, PATCH, 2 * PATCH), BF16)
 
     @pl.when(owner)
     def _():
@@ -229,7 +272,10 @@
 
     @pl.when(owner)
     def _():
-        send_strip.wait_recv()
+        @pl.when(has_up)
+        def _():
+            send_strip.wait_recv()
+
         inside = jnp.where(t == 7, PATCH, 2 * PATCH)
         rows = lax.broadcasted_iota(jnp.int32, (PATCH, 2 * PATCH), 0)
         cols = lax.broadcasted_iota(jnp.int32, (PATCH, 2 * PATCH), 1)
@@ -258,6 +304,9 @@
     def _():
         pat_pair.wait_recv()
         send_patch.wait_recv()
+
+    @pl.when(sends_strip)
+    def _():
         send_strip.wait_send()
 
     def far_rows(m, b):
@@ -392,24 +441,32 @@
     placed = mm(place_r[...], moved).astype(BF16)
     canvas[...] = mm(placed, place_c[...]).astype(BF16)
 
-    for step in range(16):
-        mode = (j + step) % 16
+    for dz, dy in FAR_FIRST:
+        mode = ((z + dz) % 4) * 4 + (y + dy) % 4
         src = canvas.at[pl.ds(pl.multiple_of(mode * SLAB, SLAB), SLAB), :]
         dst = slabs.at[c * 8 + slot]
-        if step == 0:
+
+        @pl.when(far_slabs)
+        def _():
+            to(src, slabs.at[16 + c * 8 + slot], slab_send, slab_recv.at[1], s_tile + 1, mode).start()
+
+        if (dz, dy) == (0, 0):
             @pl.when(owner)
             def _():
-                pltpu.make_async_copy(src, dst, slab_recv).start()
+                pltpu.make_async_copy(src, dst, slab_recv.at[0]).start()
 
             @pl.when(jnp.logical_not(owner))
             def _():
-                to(src, dst, slab_send, slab_recv, s_tile, mode).start()
+                to(src, dst, slab_send, slab_recv.at[0], s_tile, mode).start()
         else:
-            to(src, dst, slab_send, slab_recv, s_tile, mode).start()
+            to(src, dst, slab_send, slab_recv.at[0], s_tile, mode).start()
+
+    @pl.when(to_prev_x)
+    def _():
+        info_next.wait_recv()
 
     @pl.when(c == 0)
     def _():
-        info_next.wait_recv()
         info[4] = info[2]
 
     @pl.when(c == 1)
@@ -431,88 +488,99 @@
         cover += part if k == 0 else part * from_above
     share = 1.0 / jnp.maximum(cover, 1.0)
 
-    pltpu.make_async_copy(slabs, slabs, slab_recv).wait()
     at_row = lax.broadcasted_iota(jnp.int32, (SLAB, PATCH), 0) + j * SLAB
     at_col = lax.broadcasted_iota(jnp.int32, (SLAB, PATCH), 1)
-    own = []
-    for ri in range(2):
+
+    def gathered(which, table, ri):
         parts = [jnp.zeros((SLAB, PATCH), F32) for _ in range(4)]
         for i in range(8):
-            value = slabs[ri * 8 + i].astype(F32)
-            in_strip = at_row >= info[0, i:i + 1, 0:1]
-            in_left = at_col >= info[0, i:i + 1, 1:2]
+            value = slabs[which * 16 + ri * 8 + i].astype(F32)
+            in_strip = at_row >= info[table, i:i + 1, 0:1]
+            in_left = at_col >= info[table, i:i + 1, 1:2]
             left = jnp.where(in_left, value, 0.0)
             right = value - left
             left_own = jnp.where(in_strip, left, 0.0)
             right_own = jnp.where(in_strip, right, 0.0)
             for p, term in enumerate((left_own, right_own, left - left_own, right - right_own)):
                 parts[p] += term
-        own.append(jnp.concatenate(parts[0:2], axis=1))
-        spill[ri] = jnp.concatenate(parts[2:4], axis=1).astype(BF16)
-
-    spill_copy = to(spill, spill_in, spill_sem.at[0], spill_sem.at[1], up_tile, j)
-    spill_copy.start()
-    spill_copy.wait()
-    ring_y[y] = ((own[0] + spill_in[0].astype(F32) * from_above) * share).astype(BF16)
-    ring_z[z] = ((own[1] + spill_in[1].astype(F32) * from_above) * share).astype(BF16)
-
-    for k in range(1, 4):
-        to(ring_y.at[y], ring_y.at[y], ring_send.at[0], ring_recv.at[0], t, 4 * z + (y + k) % 4).start()
-        to(ring_z.at[z], ring_z.at[z], ring_send.at[1], ring_recv.at[1], t, 4 * ((z + k) % 4) + y).start()
-    keep = (
-        pltpu.make_async_copy(ring_y, out_hbm.at[0, z], local_sem.at[4]),
-        pltpu.make_async_copy(ring_z, out_hbm.at[1, :, y], local_sem.at[5]),
-    )
-    three = ring_y.at[pl.ds(0, 3)]
-    for p in range(2):
-        pltpu.make_async_copy(three, three, ring_recv.at[p]).wait()
-        for k in range(1, 4):
-            if p == 0:
-                to(ring_y, out_hbm.at[0, z], ring_send.at[2], ring_recv.at[2], t, 4 * ((z + k) % 4) + y).start()
-            else:
-                to(ring_z, out_hbm.at[1, :, y], ring_send.at[3], ring_recv.at[3], t, 4 * z + (y + k) % 4).start()
-        keep[p].start()
+        return jnp.concatenate(parts[0:2], axis=1), jnp.concatenate(parts[2:4], axis=1)
+
+    first16 = slabs.at[pl.ds(0, 16)]
+    pltpu.make_async_copy(first16, first16, slab_recv.at[0]).wait()
+    spill_copy = to(spill, spill_in, spill_sem.at[0], spill_sem.at[1], partner, j)
+    sums = [gathered(0, 0, ri) for ri in range(2)]
+    for ri in range(2):
+        own[ri] = sums[ri][0]
+
+    @pl.when(c == 0)
+    def _():
+        for ri in range(2):
+            spill[ri] = sums[ri][1].astype(BF16)
+        spill_copy.start()
+
+    @pl.when(to_prev_x)
+    def _():
+        pltpu.make_async_copy(first16, first16, slab_recv.at[1]).wait()
+        for ri in range(2):
+            own[ri] += gathered(1, 2, ri)[1]
+
+    @pl.when(c == 1)
+    def _():
+        spill_copy.wait_recv()
+        for ri in range(2):
+            own[ri] += spill_in[ri].astype(F32)
+
+    my_rows = out_hbm.at[:, pl.ds(pl.multiple_of(j * SLAB, SLAB), SLAB), :]
+    for ri in range(2):
+        quot[ri] = (own[ri] * share).astype(BF16)
+    for dz, dy in FAR_FIRST[:15]:
+        to(quot, my_rows, quot_send, quot_recv, t, ((z + dz) % 4) * 4 + (y + dy) % 4).start()
+    keep = pltpu.make_async_copy(quot, my_rows, local_sem.at[4])
+    keep.start()
 
     info_pair.wait_send()
 
-    @pl.when(c == 1)
+    @pl.when(to_next_x)
     def _():
         info_next.wait_send()
 
-    for here, count in ((owner, 43), (jnp.logical_not(owner), 17)):
+    @pl.when(c == 0)
+    def _():
+        spill_copy.wait_send()
+
+    for here, count in ((owner, 45), (jnp.logical_not(owner), 15)):
         @pl.when(here)
         def _():
             rows = far.at[pl.ds(0, count * 64), :]
             pltpu.make_async_copy(rows, rows, gather_send).wait()
 
-    for here, count in ((owner, 15), (jnp.logical_not(owner), 16)):
-        @pl.when(here)
-        def _():
-            rows = slabs.at[pl.ds(0, count)]
-            pltpu.make_async_copy(rows, rows, slab_send).wait()
-
-    rings = strip.at[0, pl.ds(0, 96), :]
-    for p in range(2):
-        pltpu.make_async_copy(three, three, ring_send.at[p]).wait()
-        pltpu.make_async_copy(rings, rings, ring_send.at[2 + p]).wait()
-        pltpu.make_async_copy(rings, rings, ring_recv.at[2 + p]).wait()
-        keep[p].wait()
+    for is_owner in (0, 1):
+        for is_far in (0, 1):
+            @pl.when((owner == (is_owner == 1)) & (far_slabs == (is_far == 1)))
+            def _():
+                rows = slabs.at[pl.ds(0, 16 - is_owner + 16 * is_far)]
+                pltpu.make_async_copy(rows, rows, slab_send).wait()
+
+    rows = strip.at[0, pl.ds(0, 15 * SLAB), :]
+    pltpu.make_async_copy(rows, rows, quot_send).wait()
+    pltpu.make_async_copy(rows, rows, quot_recv).wait()
+    keep.wait()
 
 
 def shards(object_field, probe_modes, patterns, offsets, counts):
     tables = jnp.asarray(make_tables())
-    any_space = pl.BlockSpec(memory_space=pl.ANY)
+    in_hbm = pl.BlockSpec(memory_space=pltpu.HBM)
     vmem = pltpu.VMEM
     dma = pltpu.SemaphoreType.DMA
     change = pl.pallas_call(
         kernel,
-        out_shape=jax.ShapeDtypeStruct((2, 4, 4, SLAB, 2 * PATCH), BF16),
+        out_shape=jax.ShapeDtypeStruct((2, PATCH, 2 * PATCH), BF16),
         in_specs=[
-            any_space, any_space, any_space, any_space,
-            pl.BlockSpec(memory_space=vmem),
+            in_hbm, in_hbm, in_hbm, in_hbm,
+            pl.BlockSpec(memory_space=pltpu.SMEM),
             pl.BlockSpec(memory_space=pltpu.SMEM),
         ],
-        out_specs=any_space,
+        out_specs=pl.BlockSpec(memory_space=pl.ANY),
         scratch_shapes=[
             vmem((2, PATCH, PATCH), F32),
             vmem((2, PATCH, 2 * PATCH), F32),
@@ -541,20 +609,20 @@
             vmem((PATCH, PATCH), BF16),
             vmem((PATCH, PATCH), BF16),
             vmem((PATCH, PATCH), BF16),
-            vmem((16, SLAB, PATCH), BF16),
+            vmem((32, SLAB, PATCH), BF16),
             vmem((2, SLAB, 2 * PATCH), BF16),
             vmem((2, SLAB, 2 * PATCH), BF16),
-            vmem((4, SLAB, 2 * PATCH), BF16),
-            vmem((4, SLAB, 2 * PATCH), BF16),
-            dma((6,)), dma, dma((8, 2, 2)), dma((2,)), dma((4,)), dma((2,)), dma((2,)),
-            dma((5,)), dma((5,)), dma, dma, dma((2,)), dma((4,)), dma((4,)),
+            vmem((2, SLAB, 2 * PATCH), F32),
+            vmem((2, SLAB, 2 * PATCH), BF16),
+            dma((5,)), dma, dma((8, 2, 2)), dma((2,)), dma((4,)), dma((2,)), dma((2,)),
+            dma((5,)), dma((5,)), dma, dma((2,)), dma((2,)), dma, dma,
         ],
         compiler_params=pltpu.CompilerParams(
-            collective_id=0, has_side_effects=True, vmem_limit_bytes=60 * 1024 * 1024
+            collective_id=0, has_side_effects=True, vmem_limit_bytes=40 * 1024 * 1024
         ),
         cost_estimate=pl.CostEstimate(flops=6 * 10**9, bytes_accessed=8 * 2**20, transcendentals=131072),
-    )(object_field, probe_modes, patterns, tables, offsets, counts)
-    return object_field + change.reshape(object_field.shape).astype(F32)
+    )(object_field, probe_modes, patterns, tables, offsets.T, counts)
+    return object_field + change.astype(F32)
 
 
 def solution(mesh):

time: 64.5 us -> 63.6 us (0.986)
  the two profiles are of different devices: /device:TPU:0 before, /device:TPU:6 now
where the time goes in v2:
time: 63.6 us; the launch traced here: 63 us
  Pallas kernels  56 us (88%)
  local copies, waits for them, and re-layouts  5.2 us (8%)
  other arithmetic  1.16 us (2%)
  between operations  0.67 us (1%)
    pallas_call x1, Pallas kernels, shards(): pl.pallas_call(kernel, out_shape=jax.ShapeDtypeStruct((2, PATCH, 2 * PATC...  56 us
    unnamed x10, local copies, waits for them, and re-layouts  5.2 us

profile of v2, /device:TPU:6, one launch (start us, length us, event | category | flops | bytes accessed | tf_op | source)
XLA Modules:
  0.0 63.0 jit_solution(17355822883459477582)
XLA Ops:
  0.7 0.0 copy-start.3
  0.7 0.7 %copy-done.3 = s32[8,2]{0,1:T(2,128)S(1)} copy-done((s32[8,2]{0,1:T(2,128)S(1)}, s32[8,2]{0,1:T(2,128)}, u32[]{:S(2)}) %copy-start.3) | copy-done | bytes 88
  1.3 0.0 copy-start
  1.3 1.2 %copy-done = f32[2,256,512]{2,1,0:T(8,128)S(1)} copy-done((f32[2,256,512]{2,1,0:T(8,128)S(1)}, f32[2,256,512]{2,1,0:T(8,128)}, u32[]{:S(2)}) %copy-start) | copy-done | bytes 1048600
  2.6 0.0 copy-start.1
  2.6 1.2 %copy-done.1 = bf16[8,256,256]{2,1,0:T(8,128)(2,1)S(1)} copy-done((bf16[8,256,256]{2,1,0:T(8,128)(2,1)S(1)}, bf16[8,256,256]{2,1,0:T(8,128)(2,1)}, u32[]{:S(2)}) %copy-start.1) | copy-done | bytes 1048600
  3.8 0.0 copy-start.2
  3.8 1.0 %copy-done.2 = f32[1,2,256,256]{3,2,1,0:T(8,128)S(1)} copy-done((f32[1,2,256,256]{3,2,1,0:T(8,128)S(1)}, f32[1,2,256,256]{3,2,1,0:T(8,128)}, u32[]{:S(2)}) %copy-start.2) | copy-done | bytes 524312
  4.8 0.0 copy-start.4
  4.8 1.0 %copy-done.4 = bf16[2,2,256,256]{3,2,1,0:T(8,128)(2,1)S(1)} copy-done((bf16[2,2,256,256]{3,2,1,0:T(8,128)(2,1)S(1)}, bf16[2,2,256,256]{3,2,1,0:T(8,128)(2,1)}, u32[]{:S(2)}) %copy-start.4) | copy-done | bytes 524312
  5.9 56.0 %shard_map.64 = bf16[2,256,512]{2,1,0:T(8,128)(2,1)S(1)} custom-call(f32[2,256,512]{2,1,0:T(8,128)S(1)} %copy-done, f32[1,2,256,256]{3,2,1,0:T(8,128)S(1)} %copy-done.2, bf16[8,256,256]{2,1,0:T(8,128)(2,1)S(1)} %copy-done.1, bf16[2,2,256,256]{3,2,1,0:T(8,128)(2,1)S(1)} %copy-done.4, s32[2,8]{1,0:T(2,128)S(1)} %bitcast.1, s32[1]{0:T(128)S(6)} %copy.7.counts_ref), custom_call_target="tpu_custom_call" | custom-call | flops 6000000000 | bytes 8388608 | tf_op jit(solution)/shard_map/pallas_call | solution.py:575
  61.9 1.2 %convert_add_fusion = f32[2,256,512]{2,1,0:T(8,128)} fusion(f32[2,256,512]{2,1,0:T(8,128)S(1)} %copy-done, bf16[2,256,512]{2,1,0:T(8,128)(2,1)S(1)} %shard_map.64), kind=kLoop, calls=%fused_computation | loop fusion | flops 524288 | bytes 2621440 | tf_op jit(solution)/shard_map/add | solution.py:625
Async XLA Ops:
  0.7 0.7 %copy-start.3 = (s32[8,2]{0,1:T(2,128)S(1)}, s32[8,2]{0,1:T(2,128)}, u32[]{:S(2)}) copy-start(s32[8,2]{0,1:T(2,128)} %param.9) | copy-start | bytes 196
  1.3 1.2 %copy-start = (f32[2,256,512]{2,1,0:T(8,128)S(1)}, f32[2,256,512]{2,1,0:T(8,128)}, u32[]{:S(2)}) copy-start(f32[2,256,512]{2,1,0:T(8,128)} %obj_hbm.1) | copy-start | bytes 3145732
  2.6 1.2 %copy-start.1 = (bf16[8,256,256]{2,1,0:T(8,128)(2,1)S(1)}, bf16[8,256,256]{2,1,0:T(8,128)(2,1)}, u32[]{:S(2)}) copy-start(bf16[8,256,256]{2,1,0:T(8,128)(2,1)} %pat_hbm.1) | copy-start | bytes 3145732
  3.8 1.0 %copy-start.2 = (f32[1,2,256,256]{3,2,1,0:T(8,128)S(1)}, f32[1,2,256,256]{3,2,1,0:T(8,128)}, u32[]{:S(2)}) copy-start(f32[1,2,256,256]{3,2,1,0:T(8,128)} %probe_hbm.1) | copy-start | bytes 1572868
  4.8 1.0 %copy-start.4 = (bf16[2,2,256,256]{3,2,1,0:T(8,128)(2,1)S(1)}, bf16[2,2,256,256]{3,2,1,0:T(8,128)(2,1)}, u32[]{:S(2)}) copy-start(bf16[2,2,256,256]{3,2,1,0:T(8,128)(2,1)} %constant.2.clone.tab_hbm) | copy-start | bytes 1572868

commit v3 on v2

--- a/solution.py
+++ b/solution.py
@@ -18,7 +18,7 @@
 BF16 = jnp.bfloat16
 F32 = jnp.float32
 
-ORDER = ((0, 0), (1, 0), (0, 1), (0, 3), (1, 1), (1, 3), (0, 2), (1, 2))
+ORDER = ((0, 0), (1, 0), (0, 1), (0, 3), (0, 2), (1, 1), (1, 3), (1, 2))
 FAR_FIRST = sorted(
     ((dz, dy) for dz in range(4) for dy in range(4)), key=lambda d: -min(d[0], 4 - d[0]) - min(d[1], 4 - d[1])
 )
@@ -47,7 +47,7 @@
 
 
 def kernel(
-    obj_hbm, probe_hbm, pat_hbm, tab_hbm, offs_ref, counts_ref, out_hbm,
+    obj_hbm, probe_hbm, pat_hbm, tab_hbm, offs_ref, counts_ref, out_ref,
     probe, strip, strip_b, ext, pat, tab, info, modes, half, far, init, cur,
     inten, ratio, upd, power, inten_b, upd_b, last_b, power_b, inten_in, upd_in, last_in, power_in,
     place_r, place_c, canvas, slabs, spill, spill_in, own, quot,
@@ -117,90 +117,6 @@
         info[2] = jnp.zeros((8, HALF), jnp.int32)
 
 
-    far_slabs = (group == 1) & (x < 3)
-    across = to_next_x | to_prev_x
-    pl.semaphore_wait(
-        barrier, 16 + jnp.where(across, 1, 0) + jnp.where(owner, 0, 16) + jnp.where(far_slabs, 16, 0)
-    )
-
-    def to(src, dst, send, recv, tile, mode):
-        return pltpu.make_async_remote_copy(
-            src_ref=src, dst_ref=dst, send_sem=send, recv_sem=recv,
-            device_id=(tile, mode), device_id_type=MESH,
-        )
-
-    info_pair = to(info.at[0], info.at[1], info_sem.at[0], info_sem.at[1], partner, j)
-    info_next = to(info.at[0], info.at[2], info_sem.at[2], info_sem.at[3], up_tile, j)
-    info_pair.start()
-
-    @pl.when(to_next_x)
-    def _():
-        info_next.start()
-
-    def block(m, s, h):
-        return modes.at[m, s, pl.ds(h * HALF, HALF), :]
-
-    def mode_slot(row, home, dy):
-        d = (row - 2 * c + 4) % 4
-        nearer = 2 * c + jnp.where((d == 1) | (d == 2), 1, 0)
-        return jnp.where(home == nearer, ORDER.index((0, dy)), ORDER.index((1, dy)))
-
-    def relay(k, s, h, home, dy, step_z, step_y):
-        row = (z + step_z + 4) % 4
-        there = mode_slot(row, home, (dy + step_y) % 4)
-        to(
-            block(k, s, h), block(there, s, h), gather_send, gather_recv.at[there, s, h],
-            t, row * 4 + (y + step_y + 4) % 4,
-        ).start()
-
-    def take(k):
-        which, dy = ORDER[k]
-        d = (z - 2 * c + 4) % 4
-        nearer = jnp.where((d == 1) | (d == 2), 1, 0)
-        home = 2 * c + (nearer if which == 0 else 1 - nearer)
-        dz = (z - home + 4) % 4
-        for h in range(2):
-            for s in range(2):
-                def wait():
-                    to(
-                        block(k, s, h), block(k, s, h), gather_send, gather_recv.at[k, s, h], t, j
-                    ).wait_recv()
-
-                if k == 0:
-                    pl.when(dz != 0)(wait)
-                else:
-                    wait()
-                if s == 0 and dy == 0:
-                    @pl.when(dz == 0)
-                    def _():
-                        for step in (2, 1, -1):
-                            relay(k, s, h, home, dy, 0, step)
-
-                if s == 1 and dy == 0:
-                    @pl.when(dz == 2)
-                    def _():
-                        relay(k, s, h, home, dy, 0, 2)
-
-                    for step in (1, -1):
-                        relay(k, s, h, home, dy, 0, step)
-                if s == 1 and (dy, h) in ((1, 0), (3, 1)):
-                    @pl.when(dz != 2)
-                    def _():
-                        relay(k, s, h, home, dy, 0, 2 - dy)
-
-                if s == 0 or dy == 0:
-                    @pl.when(dz == 0)
-                    def _():
-                        if s == 1 or dy == 2:
-                            relay(k, s, h, home, dy, 2, 0)
-                        relay(k, s, h, home, dy, 1, 0)
-                        relay(k, s, h, home, dy, -1, 0)
-
-                if s == 0 and dy != 2:
-                    @pl.when(dz == (1 if h == 0 else 3))
-                    def _():
-                        relay(k, s, h, home, dy, 1 if h == 0 else -1, 0)
-
     @pl.when(owner)
     def _():
         load_probe.wait()
@@ -213,19 +129,114 @@
             plane = mm(plane, sort_c).astype(BF16)
             for s in range(2):
                 modes[0, s, ri * HALF:(ri + 1) * HALF, :] = plane[s * HALF:(s + 1) * HALF]
-        take(0)
+
+    sends_strip = jnp.logical_not(owner) & has_down
+
+    @pl.when(sends_strip)
+    def _():
+        load_strip.wait()
+        strip_b[...] = strip[...].astype(BF16)
+
+    @pl.when(jnp.logical_not(owner | has_down))
+    def _():
+        load_strip.wait()
+
+    far_slabs = (group == 1) & (x < 3)
+    across = to_next_x | to_prev_x
+    pl.semaphore_wait(
+        barrier, 16 + jnp.where(across, 1, 0) + jnp.where(owner, 0, 16) + jnp.where(far_slabs, 16, 0)
+    )
+
+    def to(src, dst, send, recv, tile, mode):
+        return pltpu.make_async_remote_copy(
+            src_ref=src, dst_ref=dst, send_sem=send, recv_sem=recv,
+            device_id=(tile, mode), device_id_type=MESH,
+        )
+
+    info_pair = to(info.at[0], info.at[1], info_sem.at[0], info_sem.at[1], partner, j)
+    info_next = to(info.at[0], info.at[2], info_sem.at[2], info_sem.at[3], up_tile, j)
+    info_pair.start()
+
+    @pl.when(to_next_x)
+    def _():
+        info_next.start()
+
+    def block(m, s, h):
+        return modes.at[m, s, pl.ds(h * HALF, HALF), :]
+
+    def mode_slot(row, home, dy):
+        d = (row - 2 * c + 4) % 4
+        nearer = 2 * c + jnp.where((d == 1) | (d == 2), 1, 0)
+        return jnp.where(home == nearer, ORDER.index((0, dy)), ORDER.index((1, dy)))
+
+    def relay(k, s, h, home, dy, step_z, step_y):
+        row = (z + step_z + 4) % 4
+        there = mode_slot(row, home, (dy + step_y) % 4)
+        to(
+            block(k, s, h), block(there, s, h), gather_send, gather_recv.at[there, s, h],
+            t, row * 4 + (y + step_y + 4) % 4,
+        ).start()
+
+    def take(k):
+        which, dy = ORDER[k]
+        d = (z - 2 * c + 4) % 4
+        nearer = jnp.where((d == 1) | (d == 2), 1, 0)
+        home = 2 * c + (nearer if which == 0 else 1 - nearer)
+        dz = (z - home + 4) % 4
+        for h in range(2):
+            for s in range(2):
+                to(
+                    block(k, s, h), block(k, s, h), gather_send, gather_recv.at[k, s, h], t, j
+                ).wait_recv()
+                if s == 0 and dy == 0:
+                    @pl.when(dz == 0)
+                    def _():
+                        for step in (2, 1, -1):
+                            relay(k, s, h, home, dy, 0, step)
+
+                if s == 1 and dy == 0:
+                    @pl.when(dz == 2)
+                    def _():
+                        relay(k, s, h, home, dy, 0, 2)
+
+                    for step in (1, -1):
+                        relay(k, s, h, home, dy, 0, step)
+                if s == 1 and (dy, h) in ((1, 0), (3, 1)):
+                    @pl.when(dz != 2)
+                    def _():
+                        relay(k, s, h, home, dy, 0, 2 - dy)
+
+                if s == 0 or dy == 0:
+                    @pl.when(dz == 0)
+                    def _():
+                        if s == 1 or dy == 2:
+                            relay(k, s, h, home, dy, 2, 0)
+                        relay(k, s, h, home, dy, 1, 0)
+                        relay(k, s, h, home, dy, -1, 0)
+
+                if s == 0 and dy != 2:
+                    @pl.when(dz == (1 if h == 0 else 3))
+                    def _():
+                        relay(k, s, h, home, dy, 1 if h == 0 else -1, 0)
 
     send_strip = to(
         strip_b, ext.at[:, pl.ds(PATCH, PATCH), :], strip_sem.at[0], strip_sem.at[1], down_tile, j
     )
     pat_pair = to(pat_hbm.at[slot], pat, pat_sem.at[0], pat_sem.at[1], partner, j)
-    load_strip.wait()
-
-    sends_strip = jnp.logical_not(owner) & has_down
+
+    @pl.when(owner)
+    def _():
+        for h in range(2):
+            for step in (2, 1, -1):
+                relay(0, 0, h, z, 0, 0, step)
+                relay(0, 1, h, z, 0, step, 0)
+        for h in range(2):
+            for step in (1, -1):
+                relay(0, 0, h, z, 0, step, 0)
+                relay(0, 1, h, z, 0, 0, step)
 
     @pl.when(sends_strip)
     def _():
-        strip_b[...] = strip[...].astype(BF16)
         send_strip.start()
 
     @pl.when(t == 7)
@@ -235,6 +246,7 @@
     @pl.when(owner)
     def _():
         pat_pair.start()
+        load_strip.wait()
         high = strip[...].astype(BF16)
         ext[:, 0:PATCH, :] = high
         strip_b[...] = (strip[...] - high.astype(F32)).astype(BF16)
@@ -267,6 +279,9 @@
 
     place_r[...] = jnp.where((rows == wrapped(first_row + natural(cols))) & (alive > 0), 1.0, 0.0).astype(BF16)
     place_c[...] = jnp.where(cols == wrapped(first_col + natural(rows)), 1.0, 0.0).astype(BF16)
+
+    for k in range(4, 7):
+        take(k)
 
     send_patch = to(init, init, patch_sem.at[0], patch_sem.at[1], partner, j)
 
@@ -290,9 +305,6 @@
             for s in range(2):
                 init[s, ri * HALF:(ri + 1) * HALF, :] = piece[s * HALF:(s + 1) * HALF]
         send_patch.start()
-
-    for k in range(4, 6):
-        take(k)
 
     @pl.when(owner)
     def _():
@@ -385,14 +397,10 @@
     for repeat in range(PASSES):
         last = repeat == PASSES - 1
         if repeat == 0:
-            for k in range(4):
-                exit_and_left(k, init, True)
-            take(6)
-            for k in range(4, 6):
+            for k in range(7):
                 exit_and_left(k, init, True)
             take(7)
-            for k in range(6, 8):
-                exit_and_left(k, init, True)
+            exit_and_left(7, init, True)
         else:
             for k in range(8):
                 exit_and_left(k, cur, False)
@@ -530,7 +538,7 @@
         for ri in range(2):
             own[ri] += spill_in[ri].astype(F32)
 
-    my_rows = out_hbm.at[:, pl.ds(pl.multiple_of(j * SLAB, SLAB), SLAB), :]
+    my_rows = out_ref.at[:, pl.ds(pl.multiple_of(j * SLAB, SLAB), SLAB), :]
     for ri in range(2):
         quot[ri] = (own[ri] * share).astype(BF16)
     for dz, dy in FAR_FIRST[:15]:
@@ -574,13 +582,13 @@
     dma = pltpu.SemaphoreType.DMA
     change = pl.pallas_call(
         kernel,
-        out_shape=jax.ShapeDtypeStruct((2, PATCH, 2 * PATCH), BF16),
+        out_shape=vmem((2, PATCH, 2 * PATCH), BF16),
         in_specs=[
             in_hbm, in_hbm, in_hbm, in_hbm,
             pl.BlockSpec(memory_space=pltpu.SMEM),
             pl.BlockSpec(memory_space=pltpu.SMEM),
         ],
-        out_specs=pl.BlockSpec(memory_space=pl.ANY),
+        out_specs=pl.BlockSpec(memory_space=vmem),
         scratch_shapes=[
             vmem((2, PATCH, PATCH), F32),
             vmem((2, PATCH, 2 * PATCH), F32),
@@ -618,7 +626,7 @@
             dma((5,)), dma((5,)), dma, dma((2,)), dma((2,)), dma, dma,
         ],
         compiler_params=pltpu.CompilerParams(
-            collective_id=0, has_side_effects=True, vmem_limit_bytes=40 * 1024 * 1024
+            collective_id=0, has_side_effects=True, vmem_limit_bytes=56 * 1024 * 1024
         ),
         cost_estimate=pl.CostEstimate(flops=6 * 10**9, bytes_accessed=8 * 2**20, transcendentals=131072),
     )(object_field, probe_modes, patterns, tables, offsets.T, counts)

time: 63.6 us -> 57.1 us (0.90)
  local copies, waits for them, and re-layouts: 5.2 us -> 0.01 us
  Pallas kernels: 56 us -> 54.8 us
    unnamed x10 -> x2, local copies, waits for them, and re-layouts: 5.2 us -> 0.01 us
    pallas_call x1, Pallas kernels: 56 us -> 54.8 us  [shards(): pl.pallas_call(kernel, out_shape=vmem((2, PATCH, 2 * PATCH), BF16), in_sp...]
where the time goes in v3:
time: 57.1 us; the launch traced here: 56.6 us
  Pallas kernels  54.8 us (96%)
  other arithmetic  1.15 us (2%)
  between operations  0.68 us (1%)
    pallas_call x1, Pallas kernels, shards(): pl.pallas_call(kernel, out_shape=vmem((2, PATCH, 2 * PATCH), BF16), in_sp...  54.8 us
    add x1, other arithmetic, shards(): return object_field + change.astype(F32)  1.15 us

profile of v3, /device:TPU:6, one launch (start us, length us, event | category | flops | bytes accessed | tf_op | source)
XLA Modules:
  0.0 56.6 jit_solution(10105315824403857487)
XLA Ops:
  0.7 0.0 copy-start
  0.7 54.8 %shard_map.64 = bf16[2,256,512]{2,1,0:T(8,128)(2,1)S(1)} custom-call(f32[2,256,512]{2,1,0:T(8,128)} %obj_hbm.1, f32[1,2,256,256]{3,2,1,0:T(8,128)} %probe_hbm.1, bf16[8,256,256]{2,1,0:T(8,128)(2,1)} %pat_hbm.1, bf16[2,2,256,256]{3,2,1,0:T(8,128)(2,1)} %constant.2.clone.tab_hbm, s32[2,8]{1,0:T(2,128)} %bitcast.1, s32[1]{0:T(128)S(6)} %copy.7.counts_ref), custom_call_target="tpu_custom_call" | custom-call | flops 6000000000 | bytes 8388608 | tf_op jit(solution)/shard_map/pallas_call | solution.py:583
  55.4 0.0 copy-done
  55.4 1.1 %convert_add_fusion = f32[2,256,512]{2,1,0:T(8,128)} fusion(f32[2,256,512]{2,1,0:T(8,128)S(1)} %copy-done, bf16[2,256,512]{2,1,0:T(8,128)(2,1)S(1)} %shard_map.64), kind=kLoop, calls=%fused_computation | loop fusion | flops 524288 | bytes 2621440 | tf_op jit(solution)/shard_map/add | solution.py:633
Async XLA Ops:
  0.7 54.8 %copy-start = (f32[2,256,512]{2,1,0:T(8,128)S(1)}, f32[2,256,512]{2,1,0:T(8,128)}, u32[]{:S(2)}) copy-start(f32[2,256,512]{2,1,0:T(8,128)} %obj_hbm.1) | copy-start | bytes 3145732

commit v4 on v3

--- a/solution.py
+++ b/solution.py
@@ -11,6 +11,7 @@
 
 PATCH = 256
 HALF = 128
+QUARTER = 64
 PASSES = 2
 STEP_SIZE = 0.9
 SLAB = 16
@@ -96,9 +97,6 @@
     @pl.when(to_prev_x)
     def _():
         greet(down_tile, j)
-        for k in range(8):
-            for core in range(2):
-                greet(2 * x - 2 + core, 8 + k)
 
     for k in range(8):
         greet(partner, 8 * c + k)
@@ -141,10 +139,9 @@
     def _():
         load_strip.wait()
 
-    far_slabs = (group == 1) & (x < 3)
     across = to_next_x | to_prev_x
     pl.semaphore_wait(
-        barrier, 16 + jnp.where(across, 1, 0) + jnp.where(owner, 0, 16) + jnp.where(far_slabs, 16, 0)
+        barrier, 16 + jnp.where(across, 1, 0) + jnp.where(owner, 0, 16)
     )
 
     def to(src, dst, send, recv, tile, mode):
@@ -321,130 +318,180 @@
     def _():
         send_strip.wait_send()
 
-    def far_rows(m, b):
-        return pl.ds((2 * m + b) * PATCH, PATCH)
-
-    def exit_and_left(m, field, with_power):
+
+    def far_rows(m, b, r):
+        return pl.ds(((2 * m + b) * 2 + r) * HALF, HALF)
+
+    def columns(s):
+        return slice(s * HALF, (s + 1) * HALF)
+
+    def beside(parts):
+        return jnp.concatenate(parts, axis=1)
+
+    def stacked(parts):
+        return jnp.concatenate(parts, axis=0)
+
+    def exit_and_left(m):
         ends = []
         for s in range(2):
             pr = modes[m, s, 0:HALF, :].astype(F32)
             pi = modes[m, s, HALF:PATCH, :].astype(F32)
-            cr = field[s, 0:HALF, :]
-            ci = field[s, HALF:PATCH, :]
-            wave = jnp.concatenate(
-                [(pr * cr - pi * ci).astype(BF16), (pr * ci + pi * cr).astype(BF16)], axis=0
-            )
-            if with_power:
+            cr = init[s, 0:HALF, :]
+            ci = init[s, HALF:PATCH, :]
+            wave = stacked([(pr * cr - pi * ci).astype(BF16), (pr * ci + pi * cr).astype(BF16)])
+            if m == 0:
+                power[s] = pr * pr + pi * pi
+            else:
                 power[s] += pr * pr + pi * pi
             ends.append(mm(tab[0, s], wave))
         for b, part in enumerate((ends[0] + ends[1], ends[0] - ends[1])):
             part = part.astype(BF16)
             for s in range(2):
                 for ri in range(2):
-                    half[m, s, b * HALF:(b + 1) * HALF, ri * HALF:(ri + 1) * HALF] = part[
-                        ri * HALF:(ri + 1) * HALF, s * HALF:(s + 1) * HALF
+                    half[m, s, b * HALF:(b + 1) * HALF, columns(ri)] = part[
+                        ri * HALF:(ri + 1) * HALF, columns(s)
                     ]
 
-    def right_and_power(first):
-        sums = [0.0, 0.0]
-        for m in (first, first + 1):
-            even = mm(half[m, 0], tab[1, 0])
-            odd = mm(half[m, 1], tab[1, 1])
-            for b, part in enumerate((even + odd, even - odd)):
-                far[far_rows(m, b), :] = part
-                re, im = part[:, 0:HALF], part[:, HALF:PATCH]
-                sums[b] += re * re + im * im
+    def pair_probe(first, s, c2):
+        return [
+            beside([modes[m, s, columns(ri), columns(c2)] for m in (first, first + 1)]).astype(F32)
+            for ri in range(2)
+        ]
+
+    def exit_and_left_half(c2):
+        for first in range(0, 8, 2):
+            ends = []
+            for s in range(2):
+                pr, pi = pair_probe(first, s, c2)
+                cr = beside([cur[c2, s, 0:HALF, :]] * 2)
+                ci = beside([cur[c2, s, HALF:PATCH, :]] * 2)
+                wave = stacked([(pr * cr - pi * ci).astype(BF16), (pr * ci + pi * cr).astype(BF16)])
+                ends.append(mm(tab[0, s], wave))
+            for b, part in enumerate((ends[0] + ends[1], ends[0] - ends[1])):
+                part = part.astype(BF16)
+                for i in range(2):
+                    for ri in range(2):
+                        half[first + i, c2, b * HALF:(b + 1) * HALF, columns(ri)] = part[
+                            ri * HALF:(ri + 1) * HALF, columns(i)
+                        ]
+
+    def row_parts(r):
+        return slice(r * QUARTER, (r + 1) * QUARTER), slice(HALF + r * QUARTER, HALF + (r + 1) * QUARTER)
+
+    def right_and_power_half(r):
+        low, high = row_parts(r)
+        sums = [None, None]
+        for first in range(0, 8, 2):
+            ends = [
+                mm(stacked([half[m, s, rows, :] for m in (first, first + 1) for rows in (low, high)]), tab[1, s])
+                for s in range(2)
+            ]
+            for b, part in enumerate((ends[0] + ends[1], ends[0] - ends[1])):
+                for i in range(2):
+                    mine = part[i * HALF:(i + 1) * HALF]
+                    far[far_rows(first + i, b, r), :] = mine
+                    re, im = mine[:, 0:HALF], mine[:, HALF:PATCH]
+                    term = re * re + im * im
+                    sums[b] = term if sums[b] is None else sums[b] + term
         for b in range(2):
-            inten[b] = sums[b] if first == 0 else inten[b] + sums[b]
-
-    def change_and_right(m):
-        ra, rb = ratio[0], ratio[1]
-        ya = far[far_rows(m, 0), :] * jnp.concatenate([ra, ra], axis=1)
-        yb = far[far_rows(m, 1), :] * jnp.concatenate([rb, rb], axis=1)
-        for s, part in enumerate(((ya + yb).astype(BF16), (ya - yb).astype(BF16))):
-            near = mm(part, tab[0, s])
-            lo, hi = near[0:HALF], near[HALF:PATCH]
-            for b, mixed in enumerate((lo + hi, lo - hi)):
-                mixed = mixed.astype(BF16)
-                for ri in range(2):
-                    half[m, b, ri * HALF:(ri + 1) * HALF, s * HALF:(s + 1) * HALF] = mixed[
-                        :, ri * HALF:(ri + 1) * HALF
-                    ]
-
-    def left_and_update(first):
+            inten[r, b] = sums[b]
+
+    def set_ratio(repeat, r):
+        low, high = row_parts(r)
+        for b in range(2):
+            total = inten[r, b] + inten_in[repeat, r, b].astype(F32)
+            measured = stacked([pat[low, columns(b)], pat[high, columns(b)]]).astype(F32)
+            ratio[r, b] = jnp.sqrt(measured / jnp.maximum(total, 1.0)) - 1.0
+
+    def change_and_right_half(r):
+        low, high = row_parts(r)
+        for first in range(0, 8, 2):
+            plus, minus = [], []
+            for m in (first, first + 1):
+                ya = far[far_rows(m, 0, r), :] * beside([ratio[r, 0]] * 2)
+                yb = far[far_rows(m, 1, r), :] * beside([ratio[r, 1]] * 2)
+                plus.append((ya + yb).astype(BF16))
+                minus.append((ya - yb).astype(BF16))
+            for s, part in enumerate((plus, minus)):
+                near = mm(stacked(part), tab[0, s])
+                for i in range(2):
+                    lo = near[i * HALF:i * HALF + QUARTER]
+                    hi = near[i * HALF + QUARTER:(i + 1) * HALF]
+                    for b, mixed in enumerate((lo + hi, lo - hi)):
+                        mixed = mixed.astype(BF16)
+                        for ri, rows in enumerate((low, high)):
+                            half[first + i, b, rows, columns(s)] = mixed[:, columns(ri)]
+
+    def left_and_update_half(c2):
         for s in range(2):
-            re = im = 0.0
-            for m in (first, first + 1):
-                near = mm(tab[1, s], half[m, s])
+            sums = [None, None]
+            for first in range(0, 8, 2):
+                near = mm(tab[1, s], beside([half[m, s, :, columns(c2)] for m in (first, first + 1)]))
                 nr, ni = near[0:HALF], near[HALF:PATCH]
-                pr = modes[m, s, 0:HALF, :].astype(F32)
-                pi = modes[m, s, HALF:PATCH, :].astype(F32)
-                re += pr * nr + pi * ni
-                im += pr * ni - pi * nr
-            if first == 0:
-                upd[s, 0:HALF, :] = re
-                upd[s, HALF:PATCH, :] = im
-            else:
-                upd[s, 0:HALF, :] += re
-                upd[s, HALF:PATCH, :] += im
+                pr, pi = pair_probe(first, s, c2)
+                for ri, term in enumerate((pr * nr + pi * ni, pr * ni - pi * nr)):
+                    term = term[:, 0:HALF] + term[:, HALF:PATCH]
+                    sums[ri] = term if sums[ri] is None else sums[ri] + term
+            for ri in range(2):
+                upd[c2, s, columns(ri), :] = sums[ri]
 
     def swap(src, dst, which):
         copy = to(src, dst, pair_send.at[which], pair_recv.at[which], partner, j)
         copy.start()
         return copy
 
-    power[...] = jnp.zeros_like(power)
+    mine = pl.ds(pl.multiple_of(c * HALF, HALF), HALF)
+    other = pl.ds(pl.multiple_of((1 - c) * HALF, HALF), HALF)
     for repeat in range(PASSES):
-        last = repeat == PASSES - 1
         if repeat == 0:
             for k in range(7):
-                exit_and_left(k, init, True)
+                exit_and_left(k)
             take(7)
-            exit_and_left(7, init, True)
-        else:
-            for k in range(8):
-                exit_and_left(k, cur, False)
-        for k in range(0, 8, 2):
-            right_and_power(k)
-        inten_b[repeat] = inten[...].astype(BF16)
-        copy = swap(inten_b.at[repeat], inten_in.at[repeat], 3 * repeat)
+            exit_and_left(7)
+        copies = []
+        for r in range(2):
+            right_and_power_half(r)
+            inten_b[repeat, r] = inten[r].astype(BF16)
+            copies.append(swap(inten_b.at[repeat, r], inten_in.at[repeat, r], 2 * repeat + r))
         if repeat == 0:
             power_b[...] = power[...].astype(BF16)
-            power_copy = swap(power_b, power_in, 1)
-        copy.wait()
-        for b in range(2):
-            total = inten[b] + inten_in[repeat, b].astype(F32)
-            measured = pat[:, b * HALF:(b + 1) * HALF].astype(F32)
-            ratio[b] = jnp.sqrt(measured / jnp.maximum(total, 1.0)) - 1.0
-
-        for k in range(8):
-            change_and_right(k)
-        for k in range(0, 8, 2):
-            left_and_update(k)
+            power_copy = swap(power_b, power_in, 8)
+        for r in range(2):
+            copies[r].wait()
+            set_ratio(repeat, r)
+            change_and_right_half(r)
+        copies = []
+        for c2 in range(2):
+            left_and_update_half(c2)
+            if repeat < PASSES - 1:
+                upd_b[c2] = upd[c2].astype(BF16)
+                copies.append(swap(upd_b.at[c2], upd_in.at[c2], 4 + c2))
+            else:
+                last_b[c2] = upd[c2, :, other, :].astype(BF16)
+                copies.append(swap(last_b.at[c2], last_in.at[c2], 6 + c2))
         if repeat == 0:
             power_copy.wait()
             whole = power[...] + power_in[...].astype(F32)
             whole = jnp.maximum(whole[0], whole[1])
             highest = jnp.max(jnp.max(whole, axis=0, keepdims=True), axis=1, keepdims=True)
             scale = STEP_SIZE / highest
-        if not last:
-            upd_b[...] = upd[...].astype(BF16)
-            copy = swap(upd_b, upd_in, 2)
-            copy.wait()
-            for s in range(2):
-                cur[s] = init[s] + scale * (upd[s] + upd_in[s].astype(F32))
-        else:
-            mine = pl.ds(pl.multiple_of(c * HALF, HALF), HALF)
-            other = pl.ds(pl.multiple_of((1 - c) * HALF, HALF), HALF)
-            last_b[...] = upd[:, other, :].astype(BF16)
-            copy = swap(last_b, last_in, 4)
-            copy.wait()
-            moved = []
-            for s in range(2):
-                change = cur[s, mine, :] - init[s, mine, :]
-                change += scale * (upd[s, mine, :] + last_in[s].astype(F32))
-                moved.append(change.astype(BF16))
-            moved = jnp.concatenate(moved, axis=0)
+        if repeat < PASSES - 1:
+            for c2 in range(2):
+                copies[c2].wait()
+                for s in range(2):
+                    cur[c2, s] = init[s, :, columns(c2)] + scale * (upd[c2, s] + upd_in[c2, s].astype(F32))
+                exit_and_left_half(c2)
+
+    moved = []
+    for c2 in range(2):
+        copies[c2].wait()
+        column = []
+        for s in range(2):
+            change = cur[c2, s, mine, :] - init[s, mine, columns(c2)]
+            change += scale * (upd[c2, s, mine, :] + last_in[c2, s].astype(F32))
+            column.append(change.astype(BF16))
+        moved.append(stacked(column))
+    moved = beside(moved)
 
     placed = mm(place_r[...], moved).astype(BF16)
     canvas[...] = mm(placed, place_c[...]).astype(BF16)
@@ -454,20 +501,16 @@
         src = canvas.at[pl.ds(pl.multiple_of(mode * SLAB, SLAB), SLAB), :]
         dst = slabs.at[c * 8 + slot]
 
-        @pl.when(far_slabs)
-        def _():
-            to(src, slabs.at[16 + c * 8 + slot], slab_send, slab_recv.at[1], s_tile + 1, mode).start()
-
         if (dz, dy) == (0, 0):
             @pl.when(owner)
             def _():
-                pltpu.make_async_copy(src, dst, slab_recv.at[0]).start()
+                pltpu.make_async_copy(src, dst, slab_recv).start()
 
             @pl.when(jnp.logical_not(owner))
             def _():
-                to(src, dst, slab_send, slab_recv.at[0], s_tile, mode).start()
+                to(src, dst, slab_send, slab_recv, s_tile, mode).start()
         else:
-            to(src, dst, slab_send, slab_recv.at[0], s_tile, mode).start()
+            to(src, dst, slab_send, slab_recv, s_tile, mode).start()
 
     @pl.when(to_prev_x)
     def _():
@@ -513,26 +556,18 @@
                 parts[p] += term
         return jnp.concatenate(parts[0:2], axis=1), jnp.concatenate(parts[2:4], axis=1)
 
-    first16 = slabs.at[pl.ds(0, 16)]
-    pltpu.make_async_copy(first16, first16, slab_recv.at[0]).wait()
-    spill_copy = to(spill, spill_in, spill_sem.at[0], spill_sem.at[1], partner, j)
+    pltpu.make_async_copy(slabs, slabs, slab_recv).wait()
+    spill_copy = to(spill, spill_in, spill_sem.at[0], spill_sem.at[1], up_tile, j)
     sums = [gathered(0, 0, ri) for ri in range(2)]
     for ri in range(2):
+        spill[ri] = sums[ri][1].astype(BF16)
         own[ri] = sums[ri][0]
 
-    @pl.when(c == 0)
-    def _():
-        for ri in range(2):
-            spill[ri] = sums[ri][1].astype(BF16)
+    @pl.when(has_up)
+    def _():
         spill_copy.start()
 
-    @pl.when(to_prev_x)
-    def _():
-        pltpu.make_async_copy(first16, first16, slab_recv.at[1]).wait()
-        for ri in range(2):
-            own[ri] += gathered(1, 2, ri)[1]
-
-    @pl.when(c == 1)
+    @pl.when(has_down)
     def _():
         spill_copy.wait_recv()
         for ri in range(2):
@@ -552,7 +587,7 @@
     def _():
         info_next.wait_send()
 
-    @pl.when(c == 0)
+    @pl.when(has_up)
     def _():
         spill_copy.wait_send()
 
@@ -562,12 +597,11 @@
             rows = far.at[pl.ds(0, count * 64), :]
             pltpu.make_async_copy(rows, rows, gather_send).wait()
 
-    for is_owner in (0, 1):
-        for is_far in (0, 1):
-            @pl.when((owner == (is_owner == 1)) & (far_slabs == (is_far == 1)))
-            def _():
-                rows = slabs.at[pl.ds(0, 16 - is_owner + 16 * is_far)]
-                pltpu.make_async_copy(rows, rows, slab_send).wait()
+    for here, count in ((owner, 15), (jnp.logical_not(owner), 16)):
+        @pl.when(here)
+        def _():
+            rows = slabs.at[pl.ds(0, count)]
+            pltpu.make_async_copy(rows, rows, slab_send).wait()
 
     rows = strip.at[0, pl.ds(0, 15 * SLAB), :]
     pltpu.make_async_copy(rows, rows, quot_send).wait()
@@ -601,29 +635,29 @@
             vmem((8, 2, PATCH, PATCH), BF16),
             vmem((16 * PATCH, PATCH), F32),
             vmem((2, PATCH, PATCH), F32),
-            vmem((2, PATCH, PATCH), F32),
-            vmem((2, PATCH, HALF), F32),
-            vmem((2, PATCH, HALF), F32),
-            vmem((2, PATCH, PATCH), F32),
+            vmem((2, 2, PATCH, HALF), F32),
+            vmem((2, 2, HALF, HALF), F32),
+            vmem((2, 2, HALF, HALF), F32),
+            vmem((2, 2, PATCH, HALF), F32),
             vmem((2, HALF, PATCH), F32),
-            vmem((PASSES, 2, PATCH, HALF), BF16),
-            vmem((2, PATCH, PATCH), BF16),
+            vmem((PASSES, 2, 2, HALF, HALF), BF16),
+            vmem((2, 2, PATCH, HALF), BF16),
+            vmem((2, 2, HALF, HALF), BF16),
             vmem((2, HALF, PATCH), BF16),
-            vmem((2, HALF, PATCH), BF16),
-            vmem((PASSES, 2, PATCH, HALF), BF16),
-            vmem((2, PATCH, PATCH), BF16),
-            vmem((2, HALF, PATCH), BF16),
+            vmem((PASSES, 2, 2, HALF, HALF), BF16),
+            vmem((2, 2, PATCH, HALF), BF16),
+            vmem((2, 2, HALF, HALF), BF16),
             vmem((2, HALF, PATCH), BF16),
             vmem((PATCH, PATCH), BF16),
             vmem((PATCH, PATCH), BF16),
             vmem((PATCH, PATCH), BF16),
-            vmem((32, SLAB, PATCH), BF16),
+            vmem((16, SLAB, PATCH), BF16),
             vmem((2, SLAB, 2 * PATCH), BF16),
             vmem((2, SLAB, 2 * PATCH), BF16),
             vmem((2, SLAB, 2 * PATCH), F32),
             vmem((2, SLAB, 2 * PATCH), BF16),
             dma((5,)), dma, dma((8, 2, 2)), dma((2,)), dma((4,)), dma((2,)), dma((2,)),
-            dma((5,)), dma((5,)), dma, dma((2,)), dma((2,)), dma, dma,
+            dma((9,)), dma((9,)), dma, dma, dma((2,)), dma, dma,
         ],
         compiler_params=pltpu.CompilerParams(
             collective_id=0, has_side_effects=True, vmem_limit_bytes=56 * 1024 * 1024

time: 57.1 us -> 54.4 us (0.953)
  Pallas kernels: 54.8 us -> 52.4 us
    pallas_call x1, Pallas kernels: 54.8 us -> 52.4 us  [shards(): pl.pallas_call(kernel, out_shape=vmem((2, PATCH, 2 * PATCH), BF16), in_sp...]
where the time goes in v4:
time: 54.4 us; the launch traced here: 54.2 us
  Pallas kernels  52.4 us (96%)
  other arithmetic  1.15 us (2%)
  between operations  0.68 us (1%)
    pallas_call x1, Pallas kernels, shards(): pl.pallas_call(kernel, out_shape=vmem((2, PATCH, 2 * PATCH), BF16), in_sp...  52.4 us
    add x1, other arithmetic, shards(): return object_field + change.astype(F32)  1.15 us

profile of v4, /device:TPU:6, one launch (start us, length us, event | category | flops | bytes accessed | tf_op | source)
XLA Modules:
  0.0 54.2 jit_solution(10555530481821680356)
XLA Ops:
  0.7 0.0 copy-start
  0.7 52.4 %shard_map.64 = bf16[2,256,512]{2,1,0:T(8,128)(2,1)S(1)} custom-call(f32[2,256,512]{2,1,0:T(8,128)} %obj_hbm.1, f32[1,2,256,256]{3,2,1,0:T(8,128)} %probe_hbm.1, bf16[8,256,256]{2,1,0:T(8,128)(2,1)} %pat_hbm.1, bf16[2,2,256,256]{3,2,1,0:T(8,128)(2,1)} %constant.2.clone.tab_hbm, s32[2,8]{1,0:T(2,128)} %bitcast.1, s32[1]{0:T(128)S(6)} %copy.7.counts_ref), custom_call_target="tpu_custom_call" | custom-call | flops 6000000000 | bytes 8388608 | tf_op jit(solution)/shard_map/pallas_call | solution.py:617
  53.1 0.0 copy-done
  53.1 1.1 %convert_add_fusion = f32[2,256,512]{2,1,0:T(8,128)} fusion(f32[2,256,512]{2,1,0:T(8,128)S(1)} %copy-done, bf16[2,256,512]{2,1,0:T(8,128)(2,1)S(1)} %shard_map.64), kind=kLoop, calls=%fused_computation | loop fusion | flops 524288 | bytes 2621440 | tf_op jit(solution)/shard_map/add | solution.py:667
Async XLA Ops:
  0.7 52.4 %copy-start = (f32[2,256,512]{2,1,0:T(8,128)S(1)}, f32[2,256,512]{2,1,0:T(8,128)}, u32[]{:S(2)}) copy-start(f32[2,256,512]{2,1,0:T(8,128)} %obj_hbm.1) | copy-start | bytes 3145732

commit v5 on v4

--- a/solution.py
+++ b/solution.py
@@ -20,6 +20,11 @@
 F32 = jnp.float32
 
 ORDER = ((0, 0), (1, 0), (0, 1), (0, 3), (0, 2), (1, 1), (1, 3), (1, 2))
+SENT_ON_AT_HOME = (
+    (0, 1, 0), (0, 3, 0), (0, 2, 0), (1, 0, 1), (0, 1, 1), (0, 3, 1),
+    (1, 0, 0), (1, 1, 0), (1, 3, 0), (1, 1, 1), (1, 3, 1),
+)
+SENT_ON_AWAY = ((0, 0, 1), (1, 0, 1), (0, 0, 0), (0, 1, 0), (0, 3, 0), (0, 1, 1), (0, 3, 1))
 FAR_FIRST = sorted(
     ((dz, dy) for dz in range(4) for dy in range(4)), key=lambda d: -min(d[0], 4 - d[0]) - min(d[1], 4 - d[1])
 )
@@ -48,11 +53,11 @@
 
 
 def kernel(
-    obj_hbm, probe_hbm, pat_hbm, tab_hbm, offs_ref, counts_ref, out_ref,
+    obj_hbm, probe_hbm, pat_hbm, tab_hbm, offs_hbm, counts_hbm, out_ref,
     probe, strip, strip_b, ext, pat, tab, info, modes, half, far, init, cur,
     inten, ratio, upd, power, inten_b, upd_b, last_b, power_b, inten_in, upd_in, last_in, power_in,
     place_r, place_c, canvas, slabs, spill, spill_in, own, quot,
-    local_sem, gather_send, gather_recv, strip_sem, info_sem, patch_sem, pat_sem,
+    offs_ref, counts_ref, local_sem, gather_send, gather_recv, strip_sem, info_sem, patch_sem, pat_sem,
     pair_send, pair_recv, slab_send, slab_recv, spill_sem, quot_send, quot_recv,
 ):
     t = lax.axis_index("tile")
@@ -70,6 +75,11 @@
     load_strip = pltpu.make_async_copy(obj_hbm, strip, local_sem.at[1])
     load_tab = pltpu.make_async_copy(tab_hbm, tab, local_sem.at[2])
     load_pat = pltpu.make_async_copy(pat_hbm.at[slot], pat, local_sem.at[3])
+    load_offs = pltpu.make_async_copy(offs_hbm, offs_ref, local_sem.at[5])
+    load_counts = pltpu.make_async_copy(counts_hbm, counts_ref, local_sem.at[6])
+    load_offs.start()
+    load_counts.start()
+
     @pl.when(owner)
     def _():
         load_probe.start()
@@ -101,6 +111,8 @@
     for k in range(8):
         greet(partner, 8 * c + k)
 
+    load_offs.wait()
+    load_counts.wait()
     lane = lax.broadcasted_iota(jnp.int32, (8, HALF), 1)
     live = (lax.broadcasted_iota(jnp.int32, (8, HALF), 0) < counts_ref[0]).astype(jnp.int32)
     place = jnp.where(lane == 2, live, 0)
@@ -174,47 +186,55 @@
             t, row * 4 + (y + step_y + 4) % 4,
         ).start()
 
-    def take(k):
-        which, dy = ORDER[k]
+    def take(which, dy, s):
+        k = ORDER.index((which, dy))
         d = (z - 2 * c + 4) % 4
         nearer = jnp.where((d == 1) | (d == 2), 1, 0)
         home = 2 * c + (nearer if which == 0 else 1 - nearer)
         dz = (z - home + 4) % 4
         for h in range(2):
-            for s in range(2):
-                to(
-                    block(k, s, h), block(k, s, h), gather_send, gather_recv.at[k, s, h], t, j
-                ).wait_recv()
-                if s == 0 and dy == 0:
-                    @pl.when(dz == 0)
-                    def _():
-                        for step in (2, 1, -1):
-                            relay(k, s, h, home, dy, 0, step)
-
-                if s == 1 and dy == 0:
-                    @pl.when(dz == 2)
-                    def _():
-                        relay(k, s, h, home, dy, 0, 2)
-
-                    for step in (1, -1):
+            to(
+                block(k, s, h), block(k, s, h), gather_send, gather_recv.at[k, s, h], t, j
+            ).wait_recv()
+            if s == 0 and dy == 0:
+                @pl.when(dz == 0)
+                def _():
+                    for step in (2, 1, -1):
                         relay(k, s, h, home, dy, 0, step)
-                if s == 1 and (dy, h) in ((1, 0), (3, 1)):
-                    @pl.when(dz != 2)
-                    def _():
-                        relay(k, s, h, home, dy, 0, 2 - dy)
-
-                if s == 0 or dy == 0:
-                    @pl.when(dz == 0)
-                    def _():
-                        if s == 1 or dy == 2:
-                            relay(k, s, h, home, dy, 2, 0)
-                        relay(k, s, h, home, dy, 1, 0)
-                        relay(k, s, h, home, dy, -1, 0)
-
-                if s == 0 and dy != 2:
-                    @pl.when(dz == (1 if h == 0 else 3))
-                    def _():
-                        relay(k, s, h, home, dy, 1 if h == 0 else -1, 0)
+
+            if s == 1 and dy == 0:
+                @pl.when(dz == 2)
+                def _():
+                    relay(k, s, h, home, dy, 0, 2)
+
+                for step in (1, -1):
+                    relay(k, s, h, home, dy, 0, step)
+            if s == 1 and (dy, h) in ((1, 0), (3, 1)):
+                @pl.when(dz != 2)
+                def _():
+                    relay(k, s, h, home, dy, 0, 2 - dy)
+
+            if s == 0 or dy == 0:
+                @pl.when(dz == 0)
+                def _():
+                    if s == 1 or dy == 2:
+                        relay(k, s, h, home, dy, 2, 0)
+                    relay(k, s, h, home, dy, 1, 0)
+                    relay(k, s, h, home, dy, -1, 0)
+
+            if s == 0 and dy != 2:
+                @pl.when(dz == (1 if h == 0 else 3))
+                def _():
+                    relay(k, s, h, home, dy, 1 if h == 0 else -1, 0)
+
+    def finish(k):
+        which, dy = ORDER[k]
+        for here, done in ((owner, SENT_ON_AT_HOME), (jnp.logical_not(owner), SENT_ON_AWAY)):
+            @pl.when(here)
+            def _():
+                for s in range(2):
+                    if (which, dy, s) not in done and not (k == 0 and done is SENT_ON_AT_HOME):
+                        take(which, dy, s)
 
     send_strip = to(
         strip_b, ext.at[:, pl.ds(PATCH, PATCH), :], strip_sem.at[0], strip_sem.at[1], down_tile, j
@@ -223,8 +243,8 @@
 
     @pl.when(owner)
     def _():
-        for h in range(2):
-            for step in (2, 1, -1):
+        for step in (1, -1, 2):
+            for h in range(2):
                 relay(0, 0, h, z, 0, 0, step)
                 relay(0, 1, h, z, 0, step, 0)
         for h in range(2):
@@ -248,12 +268,11 @@
         ext[:, 0:PATCH, :] = high
         strip_b[...] = (strip[...] - high.astype(F32)).astype(BF16)
 
-    @pl.when(jnp.logical_not(owner))
-    def _():
-        take(0)
-
-    for k in range(1, 4):
-        take(k)
+    for here, order in ((owner, SENT_ON_AT_HOME), (jnp.logical_not(owner), SENT_ON_AWAY)):
+        @pl.when(here)
+        def _():
+            for which, dy, s in order[:5] if order is SENT_ON_AT_HOME else order:
+                take(which, dy, s)
 
     load_tab.wait()
     info_pair.wait_recv()
@@ -276,9 +295,6 @@
 
     place_r[...] = jnp.where((rows == wrapped(first_row + natural(cols))) & (alive > 0), 1.0, 0.0).astype(BF16)
     place_c[...] = jnp.where(cols == wrapped(first_col + natural(rows)), 1.0, 0.0).astype(BF16)
-
-    for k in range(4, 7):
-        take(k)
 
     send_patch = to(init, init, patch_sem.at[0], patch_sem.at[1], partner, j)
 
@@ -302,6 +318,8 @@
             for s in range(2):
                 init[s, ri * HALF:(ri + 1) * HALF, :] = piece[s * HALF:(s + 1) * HALF]
         send_patch.start()
+        for which, dy, s in SENT_ON_AT_HOME[5:]:
+            take(which, dy, s)
 
     @pl.when(owner)
     def _():
@@ -444,10 +462,9 @@
     other = pl.ds(pl.multiple_of((1 - c) * HALF, HALF), HALF)
     for repeat in range(PASSES):
         if repeat == 0:
-            for k in range(7):
+            for k in range(8):
+                finish(k)
                 exit_and_left(k)
-            take(7)
-            exit_and_left(7)
         copies = []
         for r in range(2):
             right_and_power_half(r)
@@ -619,8 +636,7 @@
         out_shape=vmem((2, PATCH, 2 * PATCH), BF16),
         in_specs=[
             in_hbm, in_hbm, in_hbm, in_hbm,
-            pl.BlockSpec(memory_space=pltpu.SMEM),
-            pl.BlockSpec(memory_space=pltpu.SMEM),
+            in_hbm, in_hbm,
         ],
         out_specs=pl.BlockSpec(memory_space=vmem),
         scratch_shapes=[
@@ -656,7 +672,8 @@
             vmem((2, SLAB, 2 * PATCH), BF16),
             vmem((2, SLAB, 2 * PATCH), F32),
             vmem((2, SLAB, 2 * PATCH), BF16),
-            dma((5,)), dma, dma((8, 2, 2)), dma((2,)), dma((4,)), dma((2,)), dma((2,)),
+            pltpu.SMEM((2, 8), jnp.int32), pltpu.SMEM((1,), jnp.int32),
+            dma((7,)), dma, dma((8, 2, 2)), dma((2,)), dma((4,)), dma((2,)), dma((2,)),
             dma((9,)), dma((9,)), dma, dma, dma((2,)), dma, dma,
         ],
         compiler_params=pltpu.CompilerParams(

time: 54.4 us -> 52.1 us (0.958)
  Pallas kernels: 52.4 us -> 49.7 us
    pallas_call x1, Pallas kernels: 52.4 us -> 49.7 us  [shards(): pl.pallas_call(kernel, out_shape=vmem((2, PATCH, 2 * PATCH), BF16), in_sp...]
where the time goes in v5:
time: 52.1 us; the launch traced here: 51.6 us
  Pallas kernels  49.7 us (95%)
  other arithmetic  1.15 us (2%)
  between operations  0.68 us (1%)
    pallas_call x1, Pallas kernels, shards(): pl.pallas_call(kernel, out_shape=vmem((2, PATCH, 2 * PATCH), BF16), in_sp...  49.7 us
    add x1, other arithmetic, shards(): return object_field + change.astype(F32)  1.15 us

profile of v5, /device:TPU:6, one launch (start us, length us, event | category | flops | bytes accessed | tf_op | source)
XLA Modules:
  0.0 51.6 jit_solution(13448384778065756428)
XLA Ops:
  0.7 0.0 copy-start
  0.7 49.7 %shard_map.64 = bf16[2,256,512]{2,1,0:T(8,128)(2,1)S(1)} custom-call(f32[2,256,512]{2,1,0:T(8,128)} %obj_hbm.1, f32[1,2,256,256]{3,2,1,0:T(8,128)} %probe_hbm.1, bf16[8,256,256]{2,1,0:T(8,128)(2,1)} %pat_hbm.1, bf16[2,2,256,256]{3,2,1,0:T(8,128)(2,1)} %constant.2.clone.tab_hbm, s32[2,8]{1,0:T(2,128)} %bitcast.1, s32[1]{0:T(128)S(6)} %copy.7.counts_hbm), custom_call_target="tpu_custom_call" | custom-call | flops 6000000000 | bytes 8388608 | tf_op jit(solution)/shard_map/pallas_call | solution.py:634
  50.4 0.0 copy-done
  50.4 1.1 %convert_add_fusion = f32[2,256,512]{2,1,0:T(8,128)} fusion(f32[2,256,512]{2,1,0:T(8,128)S(1)} %copy-done, bf16[2,256,512]{2,1,0:T(8,128)(2,1)S(1)} %shard_map.64), kind=kLoop, calls=%fused_computation | loop fusion | flops 524288 | bytes 2621440 | tf_op jit(solution)/shard_map/add | solution.py:684
Async XLA Ops:
  0.7 49.7 %copy-start = (f32[2,256,512]{2,1,0:T(8,128)S(1)}, f32[2,256,512]{2,1,0:T(8,128)}, u32[]{:S(2)}) copy-start(f32[2,256,512]{2,1,0:T(8,128)} %obj_hbm.1) | copy-start | bytes 3145732

commit v6 on v5

--- a/solution.py
+++ b/solution.py
@@ -58,7 +58,7 @@
     inten, ratio, upd, power, inten_b, upd_b, last_b, power_b, inten_in, upd_in, last_in, power_in,
     place_r, place_c, canvas, slabs, spill, spill_in, own, quot,
     offs_ref, counts_ref, local_sem, gather_send, gather_recv, strip_sem, info_sem, patch_sem, pat_sem,
-    pair_send, pair_recv, slab_send, slab_recv, spill_sem, quot_send, quot_recv,
+    pair_send, pair_recv, slab_send, slab_recv, spill_sem, quot_send, quot_recv, ring_sem, plane_sem,
 ):
     t = lax.axis_index("tile")
     j = lax.axis_index("mode")
@@ -93,8 +93,9 @@
     def greet(tile, mode):
         pl.semaphore_signal(barrier, inc=1, device_id=(tile, mode), device_id_type=MESH)
 
-    for k in range(1, 16):
-        greet(t, (j + k) % 16)
+    for k in range(1, 4):
+        greet(t, 4 * z + (y + k) % 4)
+        greet(t, 4 * ((z + k) % 4) + y)
     greet(partner, j)
     has_up, has_down = t < 7, t > 0
     to_next_x = (c == 1) & has_up
@@ -107,9 +108,6 @@
     @pl.when(to_prev_x)
     def _():
         greet(down_tile, j)
-
-    for k in range(8):
-        greet(partner, 8 * c + k)
 
     load_offs.wait()
     load_counts.wait()
@@ -152,9 +150,7 @@
         load_strip.wait()
 
     across = to_next_x | to_prev_x
-    pl.semaphore_wait(
-        barrier, 16 + jnp.where(across, 1, 0) + jnp.where(owner, 0, 16)
-    )
+    pl.semaphore_wait(barrier, 7 + jnp.where(across, 1, 0))
 
     def to(src, dst, send, recv, tile, mode):
         return pltpu.make_async_remote_copy(
@@ -255,6 +251,9 @@
     @pl.when(sends_strip)
     def _():
         send_strip.start()
+
+    for k in range(1, 4):
+        pl.semaphore_signal(ring_sem, inc=1, device_id=(t, 4 * ((z + k) % 4) + y), device_id_type=MESH)
 
     @pl.when(t == 7)
     def _():
@@ -498,6 +497,10 @@
                 for s in range(2):
                     cur[c2, s] = init[s, :, columns(c2)] + scale * (upd[c2, s] + upd_in[c2, s].astype(F32))
                 exit_and_left_half(c2)
+
+    pl.semaphore_wait(ring_sem, 3)
+    pl.semaphore_signal(plane_sem, inc=1, device_id=(partner, j), device_id_type=MESH)
+    pl.semaphore_wait(plane_sem, 1)
 
     moved = []
     for c2 in range(2):
@@ -675,6 +678,7 @@
             pltpu.SMEM((2, 8), jnp.int32), pltpu.SMEM((1,), jnp.int32),
             dma((7,)), dma, dma((8, 2, 2)), dma((2,)), dma((4,)), dma((2,)), dma((2,)),
             dma((9,)), dma((9,)), dma, dma, dma((2,)), dma, dma,
+            pltpu.SemaphoreType.REGULAR, pltpu.SemaphoreType.REGULAR,
         ],
         compiler_params=pltpu.CompilerParams(
             collective_id=0, has_side_effects=True, vmem_limit_bytes=56 * 1024 * 1024

time: 52.1 us -> 50.7 us (0.973)
  Pallas kernels: 49.7 us -> 48.5 us
    pallas_call x1, Pallas kernels: 49.7 us -> 48.5 us  [shards(): pl.pallas_call(kernel, out_shape=vmem((2, PATCH, 2 * PATCH), BF16), in_sp...]
where the time goes in v6:
time: 50.7 us; the launch traced here: 50.4 us
  Pallas kernels  48.5 us (96%)
  other arithmetic  1.15 us (2%)
  between operations  0.68 us (1%)
    pallas_call x1, Pallas kernels, shards(): pl.pallas_call(kernel, out_shape=vmem((2, PATCH, 2 * PATCH), BF16), in_sp...  48.5 us
    add x1, other arithmetic, shards(): return object_field + change.astype(F32)  1.15 us

profile of v6, /device:TPU:6, one launch (start us, length us, event | category | flops | bytes accessed | tf_op | source)
XLA Modules:
  0.0 50.4 jit_solution(11992733247308068610)
XLA Ops:
  0.7 0.0 copy-start
  0.7 48.5 %shard_map.64 = bf16[2,256,512]{2,1,0:T(8,128)(2,1)S(1)} custom-call(f32[2,256,512]{2,1,0:T(8,128)} %obj_hbm.1, f32[1,2,256,256]{3,2,1,0:T(8,128)} %probe_hbm.1, bf16[8,256,256]{2,1,0:T(8,128)(2,1)} %pat_hbm.1, bf16[2,2,256,256]{3,2,1,0:T(8,128)(2,1)} %constant.2.clone.tab_hbm, s32[2,8]{1,0:T(2,128)} %bitcast.1, s32[1]{0:T(128)S(6)} %copy.7.counts_hbm), custom_call_target="tpu_custom_call" | custom-call | flops 6000000000 | bytes 8388608 | tf_op jit(solution)/shard_map/pallas_call | solution.py:637
  49.2 0.0 copy-done
  49.2 1.1 %convert_add_fusion = f32[2,256,512]{2,1,0:T(8,128)} fusion(f32[2,256,512]{2,1,0:T(8,128)S(1)} %copy-done, bf16[2,256,512]{2,1,0:T(8,128)(2,1)S(1)} %shard_map.64), kind=kLoop, calls=%fused_computation | loop fusion | flops 524288 | bytes 2621440 | tf_op jit(solution)/shard_map/add | solution.py:688
Async XLA Ops:
  0.7 48.6 %copy-start = (f32[2,256,512]{2,1,0:T(8,128)S(1)}, f32[2,256,512]{2,1,0:T(8,128)}, u32[]{:S(2)}) copy-start(f32[2,256,512]{2,1,0:T(8,128)} %obj_hbm.1) | copy-start | bytes 3145732

commit v7 on v6

--- a/solution.py
+++ b/solution.py
@@ -22,9 +22,9 @@
 ORDER = ((0, 0), (1, 0), (0, 1), (0, 3), (0, 2), (1, 1), (1, 3), (1, 2))
 SENT_ON_AT_HOME = (
     (0, 1, 0), (0, 3, 0), (0, 2, 0), (1, 0, 1), (0, 1, 1), (0, 3, 1),
-    (1, 0, 0), (1, 1, 0), (1, 3, 0), (1, 1, 1), (1, 3, 1),
+    (1, 0, 0), (1, 1, 0), (1, 3, 0), (1, 1, 1), (1, 3, 1), (1, 2, 0),
 )
-SENT_ON_AWAY = ((0, 0, 1), (1, 0, 1), (0, 0, 0), (0, 1, 0), (0, 3, 0), (0, 1, 1), (0, 3, 1))
+SENT_ON_AWAY = ((0, 0, 1), (1, 0, 1), (0, 0, 0), (0, 1, 0), (0, 3, 0), (0, 1, 1), (0, 3, 1), (0, 2, 0))
 FAR_FIRST = sorted(
     ((dz, dy) for dz in range(4) for dy in range(4)), key=lambda d: -min(d[0], 4 - d[0]) - min(d[1], 4 - d[1])
 )
@@ -55,8 +55,8 @@
 def kernel(
     obj_hbm, probe_hbm, pat_hbm, tab_hbm, offs_hbm, counts_hbm, out_ref,
     probe, strip, strip_b, ext, pat, tab, info, modes, half, far, init, cur,
-    inten, ratio, upd, power, inten_b, upd_b, last_b, power_b, inten_in, upd_in, last_in, power_in,
-    place_r, place_c, canvas, slabs, spill, spill_in, own, quot,
+    inten, root, ratio, upd, power, inten_b, upd_b, last_b, power_b, inten_in, upd_in, last_in, power_in,
+    place_r, place_c, canvas, slabs, masks, spill, spill_in, own, quot,
     offs_ref, counts_ref, local_sem, gather_send, gather_recv, strip_sem, info_sem, patch_sem, pat_sem,
     pair_send, pair_recv, slab_send, slab_recv, spill_sem, quot_send, quot_recv, ring_sem, plane_sem,
 ):
@@ -75,18 +75,9 @@
     load_strip = pltpu.make_async_copy(obj_hbm, strip, local_sem.at[1])
     load_tab = pltpu.make_async_copy(tab_hbm, tab, local_sem.at[2])
     load_pat = pltpu.make_async_copy(pat_hbm.at[slot], pat, local_sem.at[3])
-    load_offs = pltpu.make_async_copy(offs_hbm, offs_ref, local_sem.at[5])
-    load_counts = pltpu.make_async_copy(counts_hbm, counts_ref, local_sem.at[6])
-    load_offs.start()
-    load_counts.start()
-
     @pl.when(owner)
     def _():
         load_probe.start()
-        load_pat.start()
-
-    load_strip.start()
-    load_tab.start()
 
     barrier = pltpu.get_barrier_semaphore()
 
@@ -109,21 +100,17 @@
     def _():
         greet(down_tile, j)
 
-    load_offs.wait()
-    load_counts.wait()
-    lane = lax.broadcasted_iota(jnp.int32, (8, HALF), 1)
-    live = (lax.broadcasted_iota(jnp.int32, (8, HALF), 0) < counts_ref[0]).astype(jnp.int32)
-    place = jnp.where(lane == 2, live, 0)
-    line = lax.broadcasted_iota(jnp.int32, (8, HALF), 0)
-    for i in range(8):
-        for p in range(2):
-            place = jnp.where((line == i) & (lane == p), offs_ref[p, i], place)
-    info[0] = place
-
-    @pl.when(jnp.logical_not(has_down))
-    def _():
-        info[2] = jnp.zeros((8, HALF), jnp.int32)
-
+    load_offs = pltpu.make_async_copy(offs_hbm, offs_ref, local_sem.at[5])
+    load_counts = pltpu.make_async_copy(counts_hbm, counts_ref, local_sem.at[6])
+    load_offs.start()
+    load_counts.start()
+
+    @pl.when(owner)
+    def _():
+        load_pat.start()
+
+    load_strip.start()
+    load_tab.start()
 
     @pl.when(owner)
     def _():
@@ -157,14 +144,6 @@
             src_ref=src, dst_ref=dst, send_sem=send, recv_sem=recv,
             device_id=(tile, mode), device_id_type=MESH,
         )
-
-    info_pair = to(info.at[0], info.at[1], info_sem.at[0], info_sem.at[1], partner, j)
-    info_next = to(info.at[0], info.at[2], info_sem.at[2], info_sem.at[3], up_tile, j)
-    info_pair.start()
-
-    @pl.when(to_next_x)
-    def _():
-        info_next.start()
 
     def block(m, s, h):
         return modes.at[m, s, pl.ds(h * HALF, HALF), :]
@@ -213,12 +192,12 @@
             if s == 0 or dy == 0:
                 @pl.when(dz == 0)
                 def _():
-                    if s == 1 or dy == 2:
+                    if s == 1:
                         relay(k, s, h, home, dy, 2, 0)
                     relay(k, s, h, home, dy, 1, 0)
                     relay(k, s, h, home, dy, -1, 0)
 
-            if s == 0 and dy != 2:
+            if s == 0:
                 @pl.when(dz == (1 if h == 0 else 3))
                 def _():
                     relay(k, s, h, home, dy, 1 if h == 0 else -1, 0)
@@ -252,6 +231,30 @@
     def _():
         send_strip.start()
 
+    load_offs.wait()
+    load_counts.wait()
+    lane = lax.broadcasted_iota(jnp.int32, (8, HALF), 1)
+    live = (lax.broadcasted_iota(jnp.int32, (8, HALF), 0) < counts_ref[0]).astype(jnp.int32)
+    place = jnp.where(lane == 2, live, 0)
+    line = lax.broadcasted_iota(jnp.int32, (8, HALF), 0)
+    for i in range(8):
+        for p in range(2):
+            place = jnp.where((line == i) & (lane == p), offs_ref[p, i], place)
+    info[0] = place
+
+    @pl.when(jnp.logical_not(has_down))
+    def _():
+        info[2] = jnp.zeros((8, HALF), jnp.int32)
+
+
+    info_pair = to(info.at[0], info.at[1], info_sem.at[0], info_sem.at[1], partner, j)
+    info_next = to(info.at[0], info.at[2], info_sem.at[2], info_sem.at[3], up_tile, j)
+    info_pair.start()
+
+    @pl.when(to_next_x)
+    def _():
+        info_next.start()
+
     for k in range(1, 4):
         pl.semaphore_signal(ring_sem, inc=1, device_id=(t, 4 * ((z + k) % 4) + y), device_id_type=MESH)
 
@@ -270,7 +273,7 @@
     for here, order in ((owner, SENT_ON_AT_HOME), (jnp.logical_not(owner), SENT_ON_AWAY)):
         @pl.when(here)
         def _():
-            for which, dy, s in order[:5] if order is SENT_ON_AT_HOME else order:
+            for which, dy, s in order[:8] if order is SENT_ON_AT_HOME else order:
                 take(which, dy, s)
 
     load_tab.wait()
@@ -317,7 +320,7 @@
             for s in range(2):
                 init[s, ri * HALF:(ri + 1) * HALF, :] = piece[s * HALF:(s + 1) * HALF]
         send_patch.start()
-        for which, dy, s in SENT_ON_AT_HOME[5:]:
+        for which, dy, s in SENT_ON_AT_HOME[8:]:
             take(which, dy, s)
 
     @pl.when(owner)
@@ -417,8 +420,7 @@
         low, high = row_parts(r)
         for b in range(2):
             total = inten[r, b] + inten_in[repeat, r, b].astype(F32)
-            measured = stacked([pat[low, columns(b)], pat[high, columns(b)]]).astype(F32)
-            ratio[r, b] = jnp.sqrt(measured / jnp.maximum(total, 1.0)) - 1.0
+            ratio[r, b] = root[r, b] * lax.rsqrt(jnp.maximum(total, 1.0)) - 1.0
 
     def change_and_right_half(r):
         low, high = row_parts(r)
@@ -456,6 +458,11 @@
         copy = to(src, dst, pair_send.at[which], pair_recv.at[which], partner, j)
         copy.start()
         return copy
+
+    for r in range(2):
+        low, high = row_parts(r)
+        for b in range(2):
+            root[r, b] = jnp.sqrt(stacked([pat[low, columns(b)], pat[high, columns(b)]]).astype(F32))
 
     mine = pl.ds(pl.multiple_of(c * HALF, HALF), HALF)
     other = pl.ds(pl.multiple_of((1 - c) * HALF, HALF), HALF)
@@ -562,30 +569,32 @@
     at_row = lax.broadcasted_iota(jnp.int32, (SLAB, PATCH), 0) + j * SLAB
     at_col = lax.broadcasted_iota(jnp.int32, (SLAB, PATCH), 1)
 
-    def gathered(which, table, ri):
-        parts = [jnp.zeros((SLAB, PATCH), F32) for _ in range(4)]
+    for i in range(8):
+        in_strip = at_row >= info[0, i:i + 1, 0:1]
+        in_left = at_col >= info[0, i:i + 1, 1:2]
+        for p, (kept, left) in enumerate(((True, True), (True, False), (False, True), (False, False))):
+            wanted = (in_strip if kept else jnp.logical_not(in_strip)) & (in_left if left else jnp.logical_not(in_left))
+            masks[p, i] = jnp.where(wanted, 1.0, 0.0)
+
+    def gathered(ri, past_end):
+        sums = [0.0, 0.0]
         for i in range(8):
-            value = slabs[which * 16 + ri * 8 + i].astype(F32)
-            in_strip = at_row >= info[table, i:i + 1, 0:1]
-            in_left = at_col >= info[table, i:i + 1, 1:2]
-            left = jnp.where(in_left, value, 0.0)
-            right = value - left
-            left_own = jnp.where(in_strip, left, 0.0)
-            right_own = jnp.where(in_strip, right, 0.0)
-            for p, term in enumerate((left_own, right_own, left - left_own, right - right_own)):
-                parts[p] += term
-        return jnp.concatenate(parts[0:2], axis=1), jnp.concatenate(parts[2:4], axis=1)
+            value = slabs[ri * 8 + i].astype(F32)
+            for p in range(2):
+                sums[p] += value * masks[2 * past_end + p, i]
+        return jnp.concatenate(sums, axis=1)
 
     pltpu.make_async_copy(slabs, slabs, slab_recv).wait()
     spill_copy = to(spill, spill_in, spill_sem.at[0], spill_sem.at[1], up_tile, j)
-    sums = [gathered(0, 0, ri) for ri in range(2)]
+
+    @pl.when(has_up)
+    def _():
+        for ri in range(2):
+            spill[ri] = gathered(ri, 1).astype(BF16)
+        spill_copy.start()
+
     for ri in range(2):
-        spill[ri] = sums[ri][1].astype(BF16)
-        own[ri] = sums[ri][0]
-
-    @pl.when(has_up)
-    def _():
-        spill_copy.start()
+        own[ri] = gathered(ri, 0)
 
     @pl.when(has_down)
     def _():
@@ -611,7 +620,7 @@
     def _():
         spill_copy.wait_send()
 
-    for here, count in ((owner, 45), (jnp.logical_not(owner), 15)):
+    for here, count in ((owner, 44), (jnp.logical_not(owner), 16)):
         @pl.when(here)
         def _():
             rows = far.at[pl.ds(0, count * 64), :]
@@ -657,6 +666,7 @@
             vmem((2, 2, PATCH, HALF), F32),
             vmem((2, 2, HALF, HALF), F32),
             vmem((2, 2, HALF, HALF), F32),
+            vmem((2, 2, HALF, HALF), F32),
             vmem((2, 2, PATCH, HALF), F32),
             vmem((2, HALF, PATCH), F32),
             vmem((PASSES, 2, 2, HALF, HALF), BF16),
@@ -671,6 +681,7 @@
             vmem((PATCH, PATCH), BF16),
             vmem((PATCH, PATCH), BF16),
             vmem((16, SLAB, PATCH), BF16),
+            vmem((4, 8, SLAB, PATCH), F32),
             vmem((2, SLAB, 2 * PATCH), BF16),
             vmem((2, SLAB, 2 * PATCH), BF16),
             vmem((2, SLAB, 2 * PATCH), F32),

time: 50.7 us -> 50.5 us (level)
  no operation moved by 1% of the time
where the time goes in v7:
time: 50.5 us; the launch traced here: 50.1 us
  Pallas kernels  48.3 us (96%)
  other arithmetic  1.15 us (2%)
  between operations  0.68 us (1%)
    pallas_call x1, Pallas kernels, shards(): pl.pallas_call(kernel, out_shape=vmem((2, PATCH, 2 * PATCH), BF16), in_sp...  48.3 us
    add x1, other arithmetic, shards(): return object_field + change.astype(F32)  1.15 us

profile of v7, /device:TPU:6, one launch (start us, length us, event | category | flops | bytes accessed | tf_op | source)
XLA Modules:
  0.0 50.1 jit_solution(11713669632958812941)
XLA Ops:
  0.7 0.0 copy-start
  0.7 48.3 %shard_map.64 = bf16[2,256,512]{2,1,0:T(8,128)(2,1)S(1)} custom-call(f32[2,256,512]{2,1,0:T(8,128)} %obj_hbm.1, f32[1,2,256,256]{3,2,1,0:T(8,128)} %probe_hbm.1, bf16[8,256,256]{2,1,0:T(8,128)(2,1)} %pat_hbm.1, bf16[2,2,256,256]{3,2,1,0:T(8,128)(2,1)} %constant.2.clone.tab_hbm, s32[2,8]{1,0:T(2,128)} %bitcast.1, s32[1]{0:T(128)S(6)} %copy.7.counts_hbm), custom_call_target="tpu_custom_call" | custom-call | flops 6000000000 | bytes 8388608 | tf_op jit(solution)/shard_map/pallas_call | solution.py:646
  48.9 0.0 copy-done
  49.0 1.1 %convert_add_fusion = f32[2,256,512]{2,1,0:T(8,128)} fusion(f32[2,256,512]{2,1,0:T(8,128)S(1)} %copy-done, bf16[2,256,512]{2,1,0:T(8,128)(2,1)S(1)} %shard_map.64), kind=kLoop, calls=%fused_computation | loop fusion | flops 524288 | bytes 2621440 | tf_op jit(solution)/shard_map/add | solution.py:699
Async XLA Ops:
  0.7 48.3 %copy-start = (f32[2,256,512]{2,1,0:T(8,128)S(1)}, f32[2,256,512]{2,1,0:T(8,128)}, u32[]{:S(2)}) copy-start(f32[2,256,512]{2,1,0:T(8,128)} %obj_hbm.1) | copy-start | bytes 3145732

commit v8 on v7

--- a/solution.py
+++ b/solution.py
@@ -520,24 +520,25 @@
         moved.append(stacked(column))
     moved = beside(moved)
 
-    placed = mm(place_r[...], moved).astype(BF16)
-    canvas[...] = mm(placed, place_c[...]).astype(BF16)
-
-    for dz, dy in FAR_FIRST:
-        mode = ((z + dz) % 4) * 4 + (y + dy) % 4
-        src = canvas.at[pl.ds(pl.multiple_of(mode * SLAB, SLAB), SLAB), :]
-        dst = slabs.at[c * 8 + slot]
-
-        if (dz, dy) == (0, 0):
-            @pl.when(owner)
-            def _():
-                pltpu.make_async_copy(src, dst, slab_recv).start()
-
-            @pl.when(jnp.logical_not(owner))
-            def _():
+    for dz in (2, 1, 3, 0):
+        rows = pl.ds(pl.multiple_of((z + dz) % 4 * 64, 64), 64)
+        placed = mm(place_r[rows, :], moved).astype(BF16)
+        canvas[rows, :] = mm(placed, place_c[...]).astype(BF16)
+        for dy in (2, 1, 3, 0):
+            mode = ((z + dz) % 4) * 4 + (y + dy) % 4
+            src = canvas.at[pl.ds(pl.multiple_of(mode * SLAB, SLAB), SLAB), :]
+            dst = slabs.at[c * 8 + slot]
+
+            if (dz, dy) == (0, 0):
+                @pl.when(owner)
+                def _():
+                    pltpu.make_async_copy(src, dst, slab_recv).start()
+
+                @pl.when(jnp.logical_not(owner))
+                def _():
+                    to(src, dst, slab_send, slab_recv, s_tile, mode).start()
+            else:
                 to(src, dst, slab_send, slab_recv, s_tile, mode).start()
-        else:
-            to(src, dst, slab_send, slab_recv, s_tile, mode).start()
 
     @pl.when(to_prev_x)
     def _():

time: 50.5 us -> 50.3 us (level)
  no operation moved by 1% of the time
where the time goes in v8:
time: 50.3 us; the launch traced here: 50 us
  Pallas kernels  48.2 us (96%)
  other arithmetic  1.15 us (2%)
  between operations  0.68 us (1%)
    pallas_call x1, Pallas kernels, shards(): pl.pallas_call(kernel, out_shape=vmem((2, PATCH, 2 * PATCH), BF16), in_sp...  48.2 us
    add x1, other arithmetic, shards(): return object_field + change.astype(F32)  1.15 us

profile of v8, /device:TPU:6, one launch (start us, length us, event | category | flops | bytes accessed | tf_op | source)
XLA Modules:
  0.0 50.0 jit_solution(6500284142699824593)
XLA Ops:
  0.7 0.0 copy-start
  0.7 48.2 %shard_map.64 = bf16[2,256,512]{2,1,0:T(8,128)(2,1)S(1)} custom-call(f32[2,256,512]{2,1,0:T(8,128)} %obj_hbm.1, f32[1,2,256,256]{3,2,1,0:T(8,128)} %probe_hbm.1, bf16[8,256,256]{2,1,0:T(8,128)(2,1)} %pat_hbm.1, bf16[2,2,256,256]{3,2,1,0:T(8,128)(2,1)} %constant.2.clone.tab_hbm, s32[2,8]{1,0:T(2,128)} %bitcast.1, s32[1]{0:T(128)S(6)} %copy.7.counts_hbm), custom_call_target="tpu_custom_call" | custom-call | flops 6000000000 | bytes 8388608 | tf_op jit(solution)/shard_map/pallas_call | solution.py:647
  48.9 0.0 copy-done
  48.9 1.1 %convert_add_fusion = f32[2,256,512]{2,1,0:T(8,128)} fusion(f32[2,256,512]{2,1,0:T(8,128)S(1)} %copy-done, bf16[2,256,512]{2,1,0:T(8,128)(2,1)S(1)} %shard_map.64), kind=kLoop, calls=%fused_computation | loop fusion | flops 524288 | bytes 2621440 | tf_op jit(solution)/shard_map/add | solution.py:700
Async XLA Ops:
  0.7 48.2 %copy-start = (f32[2,256,512]{2,1,0:T(8,128)S(1)}, f32[2,256,512]{2,1,0:T(8,128)}, u32[]{:S(2)}) copy-start(f32[2,256,512]{2,1,0:T(8,128)} %obj_hbm.1) | copy-start | bytes 3145732
